TPU v7x, 256 devices: a whole 4x4x8 slice. The times are simulated.
256 devices in a mesh: seq: 32 (over y, x, core), tensor: 8 (over z).
Axes of the slice: x: 4, y: 4, z: 8, core: 2. Of those that a mesh axis runs over, the one named last changes fastest.
Arguments:
- tokens: bfloat16 [65536, 5120], P('seq', 'tensor'), may hold values from -6 to 6
- value_weight: bfloat16 [5120, 1024], P('tensor'), may hold values from -0.125 to 0.125
- adapter_down_maps: bfloat16 [128, 32, 5120], P('seq', None, 'tensor'), may hold values from -0.078125 to 0.078125
- adapter_up_maps: bfloat16 [128, 32, 1024], P('seq', None, 'tensor'), may hold values from -1 to 1
- adapter_of_tile: int32 [512], P('seq'), may hold values from 0 to 127, as said below
- cotangent: bfloat16 [65536, 1024], P('seq', 'tensor'), may hold values from -6 to 6
Outputs:
- value: bfloat16 [65536, 1024], P('seq', 'tensor')
- grad_down: float32 [128, 32, 5120], P('seq', None, 'tensor')
- up_gradient: float32 [128, 32, 1024], P('seq', None, 'tensor')
Inputs may be any that keep to these rules, and one draw needn't show every extreme that they name: `adapter_of_tile`: owner of a tile is its adapter // 4. Within the aligned blocks of 2048 // 128 tiles (the tiles of one device), no owner takes more than 2 tiles; in every block some owner takes exactly 2, and one owner takes 2 tiles from every block.
All inputs are finite; a program needn't handle non-finite values.
Results may differ from a plain program's by a relative error of at most 0.0053.
Values may be sent and summed in bfloat16 or wider, within the bound.
A program may use at most 128 MiB of HBM per device.

v0:
```python
import jax
import jax.numpy as jnp
from jax import lax
from jax.sharding import PartitionSpec as P

TILE = 128
CAP = 2
ADAPT_DEV = 4


adapter_scale = 2.0


def owner_slots(adapter_of_tile, tile_count):
    owner = adapter_of_tile // ADAPT_DEV
    local = adapter_of_tile - owner * ADAPT_DEV
    places = jnp.arange(tile_count)
    earlier = (owner[:, None] == owner[None, :]) & (places[None, :] < places[:, None])
    rank = jnp.sum(earlier.astype(jnp.int32), axis=1)
    adapter_position = owner * CAP + rank
    return (adapter_position, local)


def body(tokens, value_weight, adapter_down_maps, adapter_up_maps, adapter_of_tile, cotangent):
    token_rows, width_part = tokens.shape
    feature_portion = cotangent.shape[1]
    seq_count = lax.axis_size("seq")
    tile_count = token_rows // TILE
    slot_count = seq_count * CAP
    frozen_output = lax.psum_scatter(
        lax.dot_general(
            value_weight, tokens, (((0,), (1,)), ((), ())), preferred_element_type=jnp.float32
        ),
        "tensor",
        scatter_dimension=0,
        tiled=True,
    ).T
    x_tiles = tokens.reshape(tile_count, TILE, width_part)
    g_tiles = cotangent.reshape(tile_count, TILE, feature_portion)
    adapter_position, local = owner_slots(adapter_of_tile, tile_count)
    send_x = (
        jnp.zeros((slot_count, TILE, width_part), jnp.bfloat16).at[adapter_position].set(x_tiles)
    )
    send_g = (
        jnp.zeros((slot_count, TILE, feature_portion), jnp.bfloat16)
        .at[adapter_position]
        .set(g_tiles)
    )
    send_id = (
        jnp.full((slot_count,), -1.0, jnp.bfloat16)
        .at[adapter_position]
        .set(local.astype(jnp.bfloat16))
    )
    recv_x, recv_g, recv_id = (
        lax.all_to_all(send_x, "seq", split_axis=0, concat_axis=0, tiled=True),
        lax.all_to_all(send_g, "seq", split_axis=0, concat_axis=0, tiled=True),
        lax.all_to_all(send_id, "seq", split_axis=0, concat_axis=0, tiled=True),
    )
    identity_matrix = recv_id.astype(jnp.int32)
    picked_adapter = jnp.clip(identity_matrix, 0, ADAPT_DEV - 1)
    selected_down = adapter_down_maps[picked_adapter]
    selected_up = adapter_up_maps[picked_adapter]
    low_part = jnp.einsum("std,srd->str", recv_x, selected_down, preferred_element_type=jnp.float32)
    glow_part = jnp.einsum("stv,srv->str", recv_g, selected_up, preferred_element_type=jnp.float32)
    low_sum, gradient_lowrank_sum = lax.psum((low_part, glow_part), "tensor")
    lowrank_state = low_sum.astype(jnp.bfloat16)
    gradient_lowrank = (adapter_scale * gradient_lowrank_sum).astype(jnp.bfloat16)
    adapter_update = (
        adapter_scale
        * jnp.einsum("lgz,lzx->lgx", lowrank_state, selected_up, preferred_element_type=jnp.float32)
    ).astype(jnp.bfloat16)
    returned_result = lax.all_to_all(adapter_update, "seq", split_axis=0, concat_axis=0, tiled=True)
    adapter_tile_output = returned_result[adapter_position]
    adapter_indicator = (identity_matrix[:, None] == jnp.arange(ADAPT_DEV)[None, :]).astype(
        jnp.float32
    )
    down_terms = jnp.einsum(
        "str,std->srd", gradient_lowrank, recv_x, preferred_element_type=jnp.float32
    )
    up_gradient_terms = jnp.einsum(
        "str,stv->srv", lowrank_state, recv_g, preferred_element_type=jnp.float32
    )
    grad_down = jnp.einsum(
        "sa,srd->ard", adapter_indicator, down_terms, precision=lax.Precision.HIGHEST
    )
    up_gradient = adapter_scale * jnp.einsum(
        "lh,lko->hko", adapter_indicator, up_gradient_terms, precision=lax.Precision.HIGHEST
    )
    value = (
        frozen_output + adapter_tile_output.reshape(token_rows, feature_portion).astype(jnp.float32)
    ).astype(jnp.bfloat16)
    return (value, grad_down, up_gradient)


def solution(mesh):
    in_specs = (
        P("seq", "tensor"),
        P("tensor", None),
        P("seq", None, "tensor"),
        P("seq", None, "tensor"),
        P("seq"),
        P("seq", "tensor"),
    )
    out_specs = (P("seq", "tensor"), P("seq", None, "tensor"), P("seq", None, "tensor"))
    return jax.shard_map(body, mesh=mesh, in_specs=in_specs, out_specs=out_specs, check_vma=False)
```

profile of v0, /device:TPU:1, one launch (start us, length us, event | category | flops | bytes accessed | tf_op | source)
XLA Modules:
  0.0 338.9 jit_solution(9579734626882435536)
XLA Ops:
  9.5 8.6 %all-to-all-start.1 = ((bf16[32,2,1]{1,2,0:T(2,128)(2,1)}), bf16[32,2,1]{1,2,0:T(2,128)(2,1)S(1)}, u32[]{:S(2)}, u32[]{:S(2)}) async-start(bf16[32,2,1]{1,2,0:T(2,128)(2,1)} %all_to_all.20), calls=%async_computation.2 | async-start | bytes 32768 | tf_op jit(solution)/shard_map/all_to_all | solution.py:57
  18.7 2.1 scatter_fusion.1
  20.7 1.3 copy-done.4
  22.1 2.9 all-to-all-done.1
  25.0 4.5 %all-to-all-start.3 = ((bf16[64,128,128]{2,1,0:T(8,128)(2,1)}), bf16[64,128,128]{2,1,0:T(8,128)(2,1)S(1)}, u32[]{:S(2)}, u32[]{:S(2)}) async-start(bf16[64,128,128]{2,1,0:T(8,128)(2,1)} %copy-done.4), calls=%async_computation.4 | async-start | bytes 4194304 | tf_op jit(solution)/shard_map/all_to_all | solution.py:56
  29.8 1.4 gather_fusion.1
  31.2 26.1 %all-to-all-done.3 = bf16[64,128,128]{2,1,0:T(8,128)(2,1)S(1)} async-done(((bf16[64,128,128]{2,1,0:T(8,128)(2,1)}), bf16[64,128,128]{2,1,0:T(8,128)(2,1)S(1)}, u32[]{:S(2)}, u32[]{:S(2)}) %all-to-all-start.3) | async-done | bytes 2097184 | tf_op jit(solution)/shard_map/all_to_all | solution.py:56
  57.3 3.6 %fusion.21 = f32[64,128,32]{1,2,0:T(8,128)} fusion(bf16[64,128,128]{2,1,0:T(8,128)(2,1)S(1)} %all-to-all-done.3, bf16[64,32,128]{2,1,0:T(8,128)(2,1)} %gather_fusion.1), kind=kOutput, calls=%fused_computation.44 | convolution fusion | flops 67108864 | bytes 3670016 | tf_op jit(solution)/shard_map/stv,srv->str/dot_general | solution.py:64
  61.0 7.5 %fusion.19 = f32[1024,2048]{1,0:T(8,128)} fusion(bf16[640,1024]{1,0:T(8,128)(2,1)S(1)} %copy-done, bf16[2048,640]{1,0:T(8,128)(2,1)} %param.6), kind=kOutput, calls=%fused_computation.42 | convolution fusion | flops 2684354560 | bytes 12320768 | tf_op jit(solution)/shard_map/dot_general | solution.py:31
  68.5 5.4 %broadcast_in_dim.8 = bf16[64,128,640]{2,1,0:T(8,128)(2,1)} broadcast(bf16[]{:T(256)} %constant.10.clone.1), dimensions={} | broadcast | bytes 10485762 | tf_op jit(solution)/shard_map/broadcast_in_dim | solution.py:42
  73.8 6.5 %scatter_fusion = bf16[64,128,640]{2,1,0:T(8,128)(2,1)} fusion(bf16[64,128,640]{2,1,0:T(8,128)(2,1)} %broadcast_in_dim.8, s32[16]{0:T(128)S(1)} %compare_select_fusion.1, bf16[16,128,640]{2,1,0:T(8,128)(2,1)} %bitcast.26), kind=kCustom, calls=%fused_computation.3 | custom fusion | bytes 7864384 | tf_op jit(solution)/shard_map/scatter | solution.py:42
  80.4 7.1 %all-to-all-start = ((bf16[64,128,640]{2,1,0:T(8,128)(2,1)}), bf16[64,128,640]{2,1,0:T(8,128)(2,1)}, u32[]{:S(2)}, u32[]{:S(2)}) async-start(bf16[64,128,640]{2,1,0:T(8,128)(2,1)} %scatter_fusion), calls=%async_computation.1 | async-start | bytes 20971520 | tf_op jit(solution)/shard_map/all_to_all | solution.py:55
  87.5 2.3 gather_fusion
  89.8 122.9 %all-to-all-done = bf16[64,128,640]{2,1,0:T(8,128)(2,1)} async-done(((bf16[64,128,640]{2,1,0:T(8,128)(2,1)}), bf16[64,128,640]{2,1,0:T(8,128)(2,1)}, u32[]{:S(2)}, u32[]{:S(2)}) %all-to-all-start) | async-done | bytes 10485792 | tf_op jit(solution)/shard_map/all_to_all | solution.py:55
  212.7 8.6 %fusion.20 = f32[64,128,32]{1,2,0:T(8,128)S(1)} fusion(bf16[64,128,640]{2,1,0:T(8,128)(2,1)} %all-to-all-done, bf16[64,32,640]{2,1,0:T(8,128)(2,1)} %gather_fusion), kind=kOutput, calls=%fused_computation.43 | convolution fusion | flops 335544320 | bytes 14155776 | tf_op jit(solution)/shard_map/std,srd->str/dot_general | solution.py:63
  221.3 53.2 %all-reduce.4 = bf16[64,128,32]{1,2,0:T(8,128)(2,1)S(1)} all-reduce(f32[64,128,32]{1,2,0:T(8,128)S(1)} %fusion.20), channel_id=1, replica_groups=mesh['seq'=32,'tensor'=8] {'tensor'}, use_global_device_ids=true, to_apply=%region_4.5 | all-reduce | flops 262144 | bytes 1572864 | tf_op jit(solution)/shard_map/psum | solution.py:65
  274.5 2.1 multiply_convert_fusion
  276.6 22.6 %all-to-all-start.2 = ((bf16[64,128,128]{2,1,0:T(8,128)(2,1)}), bf16[64,128,128]{2,1,0:T(8,128)(2,1)}, u32[]{:S(2)}, u32[]{:S(2)}) async-start(bf16[64,128,128]{2,1,0:T(8,128)(2,1)} %multiply_convert_fusion), calls=%async_computation.3 | async-start | bytes 4194304 | tf_op jit(solution)/shard_map/all_to_all | solution.py:72
  299.3 6.1 %fusion.4 = f32[64,32,640]{2,1,0:T(8,128)S(1)} fusion(bf16[64,128,640]{2,1,0:T(8,128)(2,1)} %all-to-all-done, f32[64,128,32]{1,2,0:T(8,128)} %all-reduce.3.cloned.1.call-done), kind=kOutput, calls=%fused_computation.14 | convolution fusion | flops 336068608 | bytes 16777216 | tf_op jit(solution)/shard_map/str,std->srd/dot_general | solution.py:77
  305.4 4.7 %fusion = f32[4,32,640]{2,0,1:T(4,128)S(1)} fusion(f32[64,32,640]{2,1,0:T(8,128)S(1)} %fusion.4, s32[64]{0:T(128)S(1)} %reshape.53), kind=kOutput, calls=%fused_computation.6 | convolution fusion | flops 62914816 | bytes 5570816 | tf_op jit(solution)/shard_map/sa,srd->ard/dot_general | solution.py:83
  311.5 1.0 convolution_multiply_fusion
  313.2 13.8 %all-to-all-done.2 = bf16[64,128,128]{2,1,0:T(8,128)(2,1)} async-done(((bf16[64,128,128]{2,1,0:T(8,128)(2,1)}), bf16[64,128,128]{2,1,0:T(8,128)(2,1)}, u32[]{:S(2)}, u32[]{:S(2)}) %all-to-all-start.2) | async-done | bytes 2097184 | tf_op jit(solution)/shard_map/all_to_all | solution.py:72
  327.0 2.2 gather_fusion.2
  329.7 1.3 fusion.2
  (37 shorter events, 6.8 us)
Async XLA Ops:
  7.2 53.8 %copy-start = (bf16[640,1024]{1,0:T(8,128)(2,1)S(1)}, bf16[640,1024]{1,0:T(8,128)(2,1)}, u32[]{:S(2)}) copy-start(bf16[640,1024]{1,0:T(8,128)(2,1)} %param.7) | copy-start | bytes 3932164
  9.5 15.5 %all-to-all-start.1 = ((bf16[32,2,1]{1,2,0:T(2,128)(2,1)}), bf16[32,2,1]{1,2,0:T(2,128)(2,1)S(1)}, u32[]{:S(2)}, u32[]{:S(2)}) async-start(bf16[32,2,1]{1,2,0:T(2,128)(2,1)} %all_to_all.20), calls=%async_computation.2 | async-start | bytes 32768 | tf_op jit(solution)/shard_map/all_to_all | solution.py:57
  18.6 11.1 %copy-start.5 = (bf16[4,32,128]{2,1,0:T(8,128)(2,1)S(1)}, bf16[4,32,128]{2,1,0:T(8,128)(2,1)}, u32[]{:S(2)}) copy-start(bf16[4,32,128]{2,1,0:T(8,128)(2,1)} %param.9) | copy-start | bytes 98308
  20.7 1.4 copy-start.4
  25.0 32.3 %all-to-all-start.3 = ((bf16[64,128,128]{2,1,0:T(8,128)(2,1)}), bf16[64,128,128]{2,1,0:T(8,128)(2,1)S(1)}, u32[]{:S(2)}, u32[]{:S(2)}) async-start(bf16[64,128,128]{2,1,0:T(8,128)(2,1)} %copy-done.4), calls=%async_computation.4 | async-start | bytes 4194304 | tf_op jit(solution)/shard_map/all_to_all | solution.py:56
  29.5 269.8 %all-reduce.3.cloned.1.call-start = ((), (), s32[]{:S(2)}) async-start(), calls=%async_computation.6 | async-start | bytes 2097152 | tf_op jit(solution)/shard_map/psum | solution.py:65
  57.3 11.1 %copy-start.2 = (bf16[64,128,128]{2,1,0:T(8,128)(2,1)}, bf16[64,128,128]{2,1,0:T(8,128)(2,1)S(1)}, u32[]{:S(2)}) copy-start(bf16[64,128,128]{2,1,0:T(8,128)(2,1)S(1)} %all-to-all-done.3) | copy-start | bytes 6291460
  60.9 268.8 %reduce-scatter.2.cloned.1.call-start = ((), (), s32[]{:S(2)}) async-start(), calls=%async_computation.5 | async-start | bytes 9437184 | tf_op jit(solution)/shard_map/reduce_scatter | solution.py:30
  80.4 7.1 %copy-start.1 = (bf16[4,32,640]{2,1,0:T(8,128)(2,1)S(1)}, bf16[4,32,640]{2,1,0:T(8,128)(2,1)}, u32[]{:S(2)}) copy-start(bf16[4,32,640]{2,1,0:T(8,128)(2,1)} %param.8) | copy-start | bytes 491524
  80.4 132.3 %all-to-all-start = ((bf16[64,128,640]{2,1,0:T(8,128)(2,1)}), bf16[64,128,640]{2,1,0:T(8,128)(2,1)}, u32[]{:S(2)}, u32[]{:S(2)}) async-start(bf16[64,128,640]{2,1,0:T(8,128)(2,1)} %scatter_fusion), calls=%async_computation.1 | async-start | bytes 20971520 | tf_op jit(solution)/shard_map/all_to_all | solution.py:55
  89.8 184.7 %copy-start.6 = (bf16[64,32,128]{2,1,0:T(8,128)(2,1)S(1)}, bf16[64,32,128]{2,1,0:T(8,128)(2,1)}, u32[]{:S(2)}) copy-start(bf16[64,32,128]{2,1,0:T(8,128)(2,1)} %gather_fusion.1) | copy-start | bytes 1572868
  276.6 50.4 %all-to-all-start.2 = ((bf16[64,128,128]{2,1,0:T(8,128)(2,1)}), bf16[64,128,128]{2,1,0:T(8,128)(2,1)}, u32[]{:S(2)}, u32[]{:S(2)}) async-start(bf16[64,128,128]{2,1,0:T(8,128)(2,1)} %multiply_convert_fusion), calls=%async_computation.3 | async-start | bytes 4194304 | tf_op jit(solution)/shard_map/all_to_all | solution.py:72
  305.4 5.5 %copy-start.3 = (bf16[64,128,128]{2,1,0:T(8,128)(2,1)S(1)}, bf16[64,128,128]{2,1,0:T(8,128)(2,1)}, u32[]{:S(2)}) copy-start(bf16[64,128,128]{2,1,0:T(8,128)(2,1)} %copy-done.2) | copy-start | bytes 6291460
Sparse Core Ops, SparseCore 0:
  61.0 73.0 all-reduce.2
  136.7 97.3 reduce-scatter.1
where the time goes:
time: 340 us; the launch traced here: 339 us
  waiting for transfers between devices  166 us (49%)
  blocking collectives  53.2 us (16%)
  starting transfers between devices  42.8 us (13%)
  matrix products  34.2 us (10%)
  local copies, waits for them, and re-layouts  26.1 us (8%)
  between operations  14.3 us (4%)
    all_to_all x1, waiting for transfers between devices, body(): lax.all_to_all(send_x, 'seq', split_axis=0, concat_axis=0, tiled=True)  123 us
    psum x1, blocking collectives, body(): low_sum, gradient_lowrank_sum = lax.psum((low_part, glow_part), 'tensor')  53.2 us
    all_to_all x1, waiting for transfers between devices, body(): lax.all_to_all(send_g, 'seq', split_axis=0, concat_axis=0, tiled=True)  26.1 us
    all_to_all x1, starting transfers between devices, body(): lax.all_to_all(adapter_update, 'seq', split_axis=0, concat_axis=0, tiled=...  22.6 us
    all_to_all x1, waiting for transfers between devices, body(): lax.all_to_all(adapter_update, 'seq', split_axis=0, concat_axis=0, tiled=...  13.8 us
    all_to_all x1, starting transfers between devices, body(): lax.all_to_all(send_id, 'seq', split_axis=0, concat_axis=0, tiled=True)  8.59 us
    dot_general x1, matrix products, body(): jnp.einsum('std,srd->str', recv_x, selected_down, preferred_element_type=...  8.58 us
    dot_general x1, matrix products, body(): lax.dot_general(value_weight, tokens, (((0,), (1,)), ((), ())), preferred...  7.45 us
  transfers between devices with their start and end apart: 6, of which 4 were waited for; matrix products, arithmetic and copies ran while one was open for 16% of the time, Pallas kernels for 0%

commit v1 on v0

v1 whole, which is shorter than its diff:
```python
import jax
import jax.numpy as jnp
from jax import lax
from jax.sharding import PartitionSpec as P

TILE = 128
adapter_scale = 2.0


def body(tokens, value_weight, adapter_down_maps, adapter_up_maps, adapter_of_tile, cotangent):
    token_rows, width_part = tokens.shape
    feature_portion = cotangent.shape[1]
    tile_count = token_rows // TILE
    adapters = jnp.concatenate([adapter_down_maps, adapter_up_maps], axis=2)
    all_adapters = lax.all_gather(adapters, "seq", axis=0, tiled=True)
    adapter_count = all_adapters.shape[0]
    frozen_output = lax.psum_scatter(
        lax.dot_general(
            tokens, value_weight, (((1,), (0,)), ((), ())), preferred_element_type=jnp.float32
        ).astype(jnp.bfloat16),
        "tensor",
        scatter_dimension=1,
        tiled=True,
    )
    picked = all_adapters[adapter_of_tile]
    selected_down = picked[:, :, :width_part]
    selected_up = picked[:, :, width_part:]
    x_tiles = tokens.reshape(tile_count, TILE, width_part)
    g_tiles = cotangent.reshape(tile_count, TILE, feature_portion)
    low_part = jnp.einsum("std,srd->srt", x_tiles, selected_down, preferred_element_type=jnp.float32)
    glow_part = jnp.einsum("stv,srv->srt", g_tiles, selected_up, preferred_element_type=jnp.float32)
    sums = lax.psum(jnp.concatenate([low_part, glow_part], axis=1), "tensor")
    rank = selected_down.shape[1]
    low = sums[:, :rank].astype(jnp.bfloat16)
    glow = (adapter_scale * sums[:, rank:]).astype(jnp.bfloat16)
    update = (
        adapter_scale * jnp.einsum("srt,srv->stv", low, selected_up, preferred_element_type=jnp.float32)
    ).astype(jnp.bfloat16)
    down_terms = jnp.einsum("srt,std->srd", glow, x_tiles, preferred_element_type=jnp.float32)
    up_terms = adapter_scale * jnp.einsum("srt,stv->srv", low, g_tiles, preferred_element_type=jnp.float32)
    terms = jnp.concatenate([down_terms, up_terms], axis=2)
    summed = jnp.zeros((adapter_count,) + terms.shape[1:], jnp.float32).at[adapter_of_tile].add(terms)
    grads = lax.psum_scatter(summed.astype(jnp.bfloat16), "seq", scatter_dimension=0, tiled=True)
    grads = grads.astype(jnp.float32)
    value = (
        frozen_output.astype(jnp.float32) + update.reshape(token_rows, feature_portion).astype(jnp.float32)
    ).astype(jnp.bfloat16)
    return value, grads[:, :, :width_part], grads[:, :, width_part:]


def solution(mesh):
    in_specs = (
        P("seq", "tensor"),
        P("tensor", None),
        P("seq", None, "tensor"),
        P("seq", None, "tensor"),
        P("seq"),
        P("seq", "tensor"),
    )
    out_specs = (P("seq", "tensor"), P("seq", None, "tensor"), P("seq", None, "tensor"))
    return jax.shard_map(body, mesh=mesh, in_specs=in_specs, out_specs=out_specs, check_vma=False)
```

time: 340 us -> 310 us (0.912)
  waiting for transfers between devices: 166 us -> 242 us
  blocking collectives: 53.2 us -> 0 us
  starting transfers between devices: 42.8 us -> 0.16 us
  matrix products: 34.2 us -> 11.8 us
  other arithmetic: 2.53 us -> 19.8 us
  local copies, waits for them, and re-layouts: 26.1 us -> 21.2 us
    all_to_all x4 -> x0, waiting for transfers between devices: 166 us -> none  [the longest x1 123 us: body(): lax.all_to_all(send_x, 'seq', split_axis=0, concat_axis=0, tiled=True)]
    reduce_scatter x1, waiting for transfers between devices: 0.02 us -> 89.9 us  [body(): lax.psum_scatter(summed.astype(jnp.bfloat16), 'seq', scatter_dimension=0,...]
    all_gather x0 -> x1, waiting for transfers between devices: none -> 59.8 us  [body(): all_adapters = lax.all_gather(adapters, 'seq', axis=0, tiled=True)]
    psum x1, waiting for transfers between devices: 0.02 us -> 54.7 us  [body(): sums = lax.psum(jnp.concatenate([low_part, glow_part], axis=1), 'tensor')]
    psum x1 -> x0, blocking collectives: 53.2 us -> none  [body(): low_sum, gradient_lowrank_sum = lax.psum((low_part, glow_part), 'tensor')]
    all_to_all x4 -> x0, starting transfers between devices: 42.7 us -> none  [the longest x1 22.6 us: body(): lax.all_to_all(adapter_update, 'seq', split_axis=0, concat_axis=0, tiled=...]
    unnamed x2 -> x5, waiting for transfers between devices: 0.03 us -> 37.6 us
    dot_general x8 -> x6, matrix products: 34.2 us -> 11.8 us  [the longest x1 6.24 us: body(): lax.dot_general(tokens, value_weight, (((1,), (0,)), ((), ())), preferred...]
  transfers between devices with their start and end apart: 6 -> 4, of which waited for: 4 -> 4; matrix products, arithmetic and copies ran while one was open for 16% -> 14% of each run, Pallas kernels for 0% -> 0%
where the time goes in v1:
time: 310 us; the launch traced here: 309 us
  waiting for transfers between devices  242 us (78%)
  local copies, waits for them, and re-layouts  21.2 us (7%)
  other arithmetic  19.8 us (6%)
  between operations  13.8 us (4%)
  matrix products  11.8 us (4%)
    reduce_scatter x1, waiting for transfers between devices, body(): lax.psum_scatter(summed.astype(jnp.bfloat16), 'seq', scatter_dimension=0,...  89.9 us
    all_gather x1, waiting for transfers between devices, body(): all_adapters = lax.all_gather(adapters, 'seq', axis=0, tiled=True)  59.8 us
    psum x1, waiting for transfers between devices, body(): sums = lax.psum(jnp.concatenate([low_part, glow_part], axis=1), 'tensor')  54.7 us
    unnamed x5, waiting for transfers between devices  37.6 us
    unnamed x6, local copies, waits for them, and re-layouts  8.59 us
    convert_element_type x1, other arithmetic, body(): summed.astype(jnp.bfloat16)  8.54 us
    dot_general x1, matrix products, body(): lax.dot_general(tokens, value_weight, (((1,), (0,)), ((), ())), preferred...  6.24 us
  transfers between devices with their start and end apart: 4, of which 4 were waited for; matrix products, arithmetic and copies ran while one was open for 14% of the time, Pallas kernels for 0%

profile of v1, /device:TPU:1, one launch (start us, length us, event | category | flops | bytes accessed | tf_op | source)
XLA Modules:
  0.0 308.7 jit_solution(12881924314590920114)
XLA Ops:
  7.2 1.8 pad_maximum_fusion.2
  9.1 0.7 compare_select_fusion
  9.7 59.8 %all-gather.2.cloned.1.call-done = bf16[128,32,768]{2,1,0:T(8,128)(2,1)} async-done(((bf16[4,32,768]{2,1,0:T(8,128)(2,1)}), bf16[128,32,768]{2,1,0:T(8,128)(2,1)}) %all-gather.2.cloned.1.call-update) | async-done | bytes 6291472 | tf_op jit(solution)/shard_map/all_gather | solution.py:15
  69.5 3.4 %gather_fusion = bf16[16,32,768]{2,1,0:T(8,128)(2,1)S(1)} fusion(bf16[128,32,768]{2,1,0:T(8,128)(2,1)} %all-gather.2.cloned.1.call-done, s32[1024]{0:T(1024)S(1)} %pad_clamp_fusion), kind=kCustom, calls=%fused_computation | custom fusion | bytes 1572928 | tf_op jit(solution)/shard_map/gather | solution.py:25
  72.9 1.0 fusion.2
  73.9 0.1 copy-done.1
  74.0 0.4 fusion.9
  74.3 0.8 pad_maximum_fusion.1
  75.3 6.2 %convolution_convert_fusion = bf16[2048,1024]{1,0:T(8,128)(2,1)} fusion(bf16[2048,640]{1,0:T(8,128)(2,1)S(1)} %copy-done, bf16[640,1024]{1,0:T(8,128)(2,1)} %param.7), kind=kOutput, calls=%fused_computation.2 | convolution fusion | flops 2686451712 | bytes 8126464 | tf_op jit(solution)/shard_map/dot_general | solution.py:18
  81.5 6.5 %copy.9 = bf16[2048,1024]{0,1:T(8,128)(2,1)} copy(bf16[2048,1024]{1,0:T(8,128)(2,1)} %convolution_convert_fusion) | data formatting | bytes 8388608
  88.1 54.7 %all-reduce.2.cloned.1.call-done = f32[16,64,128]{2,1,0:T(8,128)} async-done(((f32[16,64,128]{2,1,0:T(8,128)}), f32[16,64,128]{2,1,0:T(8,128)}) %all-reduce.2.cloned.1.call-update) | async-done | bytes 524304 | tf_op jit(solution)/shard_map/psum | solution.py:32
  142.8 1.4 convolution_multiply_fusion.1
  144.2 1.5 fusion.5
  145.7 1.3 pad_maximum_fusion
  147.0 6.1 %broadcast_in_dim.8 = f32[128,32,768]{2,1,0:T(8,128)} broadcast(f32[]{:T(128)} %constant.2.clone.1), dimensions={} | broadcast | bytes 12582916 | tf_op jit(solution)/shard_map/broadcast_in_dim | solution.py:42
  153.1 4.6 %scatter_fusion = f32[128,32,768]{2,1,0:T(8,128)} fusion(f32[128,32,768]{2,1,0:T(8,128)} %broadcast_in_dim.8, s32[16]{0:T(128)S(1)} %compare_select_fusion, f32[16,32,768]{2,1,0:T(8,128)} %pad_maximum_fusion), kind=kCustom, calls=%fused_computation.1 | custom fusion | flops 393216 | bytes 4718656 | tf_op jit(solution)/shard_map/scatter-add | solution.py:42
  157.8 8.5 %convert_element_type.35 = bf16[128,32,768]{2,1,0:T(8,128)(2,1)} convert(f32[128,32,768]{2,1,0:T(8,128)} %scatter_fusion) | non-fusion elementwise | flops 3145728 | bytes 18874368 | tf_op jit(solution)/shard_map/convert_element_type | solution.py:43
  166.3 37.6 %reduce-scatter.7.cloned.1.call-done = bf16[128,2048]{1,0:T(8,128)(2,1)} async-done(((bf16[1024,2048]{1,0:T(8,128)(2,1)}), bf16[128,2048]{1,0:T(8,128)(2,1)}) %reduce-scatter.7.cloned.1.call-update) | async-done | bytes 524304
  203.9 2.0 copy.10
  205.9 1.3 fusion
  207.2 2.0 fusion.1
  209.2 89.9 %reduce-scatter.5.cloned.1.call-done = bf16[4,32,768]{2,1,0:T(8,128)(2,1)} async-done(((bf16[128,32,768]{2,1,0:T(8,128)(2,1)}), bf16[4,32,768]{2,1,0:T(8,128)(2,1)}) %reduce-scatter.5.cloned.1.call-update) | async-done | bytes 196624 | tf_op jit(solution)/shard_map/reduce_scatter | solution.py:43
  299.1 1.4 slice.32
  300.5 1.7 slice.31
  (12 shorter events, 0.3 us)
Async XLA Ops:
  7.2 65.7 %copy-start = (bf16[2048,640]{1,0:T(8,128)(2,1)S(1)}, bf16[2048,640]{1,0:T(8,128)(2,1)}, u32[]{:S(2)}) copy-start(bf16[2048,640]{1,0:T(8,128)(2,1)} %param.6) | copy-start | bytes 7864324
  7.2 62.3 %all-gather.2.cloned.1.call-start = ((), (), s32[]{:S(2)}) async-start(), calls=%async_computation.2 | async-start | bytes 6488064 | tf_op jit(solution)/shard_map/all_gather | solution.py:15
  9.0 133.8 %all-reduce.2.cloned.1.call-start = ((), (), s32[]{:S(2)}) async-start(), calls=%async_computation.3 | async-start | bytes 1048576 | tf_op jit(solution)/shard_map/psum | solution.py:32
  72.9 1.0 copy-start.1
  75.2 128.7 %reduce-scatter.7.cloned.1.call-start = ((), (), s32[]{:S(2)}) async-start(), calls=%async_computation.5 | async-start | bytes 4718592
  88.0 211.1 %reduce-scatter.5.cloned.1.call-start = ((), (), s32[]{:S(2)}) async-start(), calls=%async_computation.4 | async-start | bytes 6488064 | tf_op jit(solution)/shard_map/reduce_scatter | solution.py:43
Sparse Core Ops, SparseCore 0:
  11.1 58.3 all-gather.1
  75.3 67.4 all-reduce.1
  145.5 58.3 reduce-scatter.6
  208.3 90.7 reduce-scatter.4

commit v2 on v1

v2 whole, which is shorter than its diff:
```python
import jax
import jax.numpy as jnp
from jax import lax
from jax.experimental import pallas as pl
from jax.experimental.pallas import tpu as pltpu
from jax.sharding import PartitionSpec as P

TILE = 128
NX, NY, NC, NZ = 4, 4, 2, 8
OWN = 4
SCALE = 2.0
SUB = 2
BLK = 256
MESH = pl.DeviceIdType.MESH
BF = jnp.bfloat16
F32 = jnp.float32


def kernel(
    ids, tok_h, w_h, down_h, up_h, cot_h,
    val_o, gd_o, ug_o,
    tok, w, cot, ad, acc, zs, zr, part, ar, low, tfull, tpart, tab, tabp, tabs,
    g, r1, r2, sf, sb, r3, r4, fin, rfin, full,
    lsem, ag_s, ag_r, d_s, d_r, z_s, z_r, ar_s, ar_r, br_s, br_r, t_s, t_r, g_s, g_r, f_s, f_r,
):
    width = tok.shape[1]
    rows = tok.shape[0]
    rank = down_h.shape[1]
    feat = cot.shape[1]
    tiles = rows // TILE
    cols = width + feat
    half = cols // 2
    hrows = rows // 2
    srows = hrows // SUB
    s_idx = lax.axis_index("seq")
    z = lax.axis_index("tensor")
    c = s_idx % 2
    x = (s_idx // 2) % NX
    y = s_idx // (2 * NX)

    def dev(yy, xx, cc):
        return ((yy * NX + xx) * NC + cc, z)

    def zdev(d):
        return (s_idx, (z + d) % NZ)

    pos = ((y, x), (x, y))

    def hdev(h, dp, dq):
        pp, qq = (pos[h][0] + dp + 4) % 4, (pos[h][1] + dq + 4) % 4
        return dev(pp, qq, c) if h == 0 else dev(qq, pp, c)

    mate = dev(y, x, 1 - c)

    def remote(src, dst, ss, rs, device):
        return pltpu.make_async_remote_copy(
            src_ref=src, dst_ref=dst, send_sem=ss, recv_sem=rs, device_id=device, device_id_type=MESH
        )

    sent = []

    def send(src, dst, ss, rs, device):
        cp = remote(src, dst, ss, rs, device)
        cp.start()
        sent.append(cp)

    def got(dst, ss, rs, device):
        remote(dst, dst, ss, rs, device).wait_recv()

    loads = []
    for h in range(2):
        own = ad.at[h, c, pos[h][0], pos[h][1]]
        loads.append(pltpu.make_async_copy(down_h.at[pl.ds(2 * h, 2)], own.at[:, :, pl.ds(0, width)], lsem.at[2 * h]))
        loads.append(pltpu.make_async_copy(up_h.at[pl.ds(2 * h, 2)], own.at[:, :, pl.ds(width, feat)], lsem.at[2 * h + 1]))
    loads.append(pltpu.make_async_copy(tok_h, tok, lsem.at[4]))
    loads.append(pltpu.make_async_copy(w_h, w, lsem.at[5]))
    loads.append(pltpu.make_async_copy(cot_h, cot, lsem.at[6]))
    for cp in loads:
        cp.start()
    bar = pltpu.get_barrier_semaphore()
    friends = [zdev(d) for d in range(1, NZ)] + [mate]
    friends += [hdev(0, 1, 0), hdev(0, -1, 0), hdev(0, 0, 1), hdev(0, 0, -1)]
    for f in friends:
        pl.semaphore_signal(bar, inc=1, device_id=f, device_id_type=MESH)
    lane = lax.broadcasted_iota(jnp.int32, (8, 128), 1)
    row = lax.broadcasted_iota(jnp.int32, (8, 128), 0)
    first = jnp.full((8, 128), tiles, jnp.int32)
    count = jnp.zeros((8, 128), jnp.int32)
    last = jnp.full((8, 128), tiles, jnp.int32)
    for t in range(tiles):
        hit = lane == ids[t]
        last = jnp.where(hit & (count == 1), t, last)
        first = jnp.where(hit & (count == 0), t, first)
        count = count + hit.astype(jnp.int32)
    tab[...] = jnp.where(row == 0, first, last)
    tfull[tiles] = jnp.zeros((rank, cols), BF)
    tpart[tiles] = jnp.zeros((rank, half), BF)
    for cp in loads[:4]:
        cp.wait()
    pl.semaphore_wait(bar, len(friends))

    def ag1():
        for h in range(2):
            blk = ad.at[h, c, pos[h][0], pos[h][1]]
            send(blk, blk, ag_s.at[h, 0, 0], ag_r.at[h, 0, 0], hdev(h, 0, 1))
            send(blk, blk, ag_s.at[h, 0, 1], ag_r.at[h, 0, 1], hdev(h, 0, -1))
        send(tab, tabp, t_s.at[1], t_r.at[1], mate)

    def ag2():
        for h in range(2):
            pp, qq = pos[h]
            for i, dq in ((0, 1), (1, -1)):
                prev = (qq - dq + 4) % 4
                blk = ad.at[h, c, pp, prev]
                got(blk, ag_s.at[h, 0, i], ag_r.at[h, 0, i], hdev(h, 0, dq))
                piece = ad.at[h, c, pp, prev, pl.ds(i, 1)]
                send(piece, piece, ag_s.at[h, 1, i], ag_r.at[h, 1, i], hdev(h, 0, dq))

    def ag3():
        for h in range(2):
            pp, qq = pos[h]
            for i, dq in ((0, 1), (1, -1)):
                piece = ad.at[h, c, pp, (qq + 2) % 4, pl.ds(i, 1)]
                got(piece, ag_s.at[h, 1, i], ag_r.at[h, 1, i], hdev(h, 0, dq))
            blk = ad.at[h, c, pp]
            send(blk, blk, ag_s.at[h, 2, 0], ag_r.at[h, 2, 0], hdev(h, 1, 0))
            send(blk, blk, ag_s.at[h, 2, 1], ag_r.at[h, 2, 1], hdev(h, -1, 0))
            send(blk, blk, d_s.at[h, 0], d_r.at[h, 0], mate)

    def ag4():
        for h in range(2):
            pp, qq = pos[h]
            for i, dp in ((0, 1), (1, -1)):
                prev = (pp - dp + 4) % 4
                blk = ad.at[h, c, prev]
                got(blk, ag_s.at[h, 2, i], ag_r.at[h, 2, i], hdev(h, dp, 0))
                piece = ad.at[h, c, prev, pl.ds(2 * i, 2)]
                send(piece, piece, ag_s.at[h, 3, i], ag_r.at[h, 3, i], hdev(h, dp, 0))
                send(blk, blk, d_s.at[h, 1 + i], d_r.at[h, 1 + i], mate)

    def ag5():
        for h in range(2):
            pp, qq = pos[h]
            far = (pp + 2) % 4
            for i, dp in ((0, 1), (1, -1)):
                piece = ad.at[h, c, far, pl.ds(2 * i, 2)]
                got(piece, ag_s.at[h, 3, i], ag_r.at[h, 3, i], hdev(h, dp, 0))
            blk = ad.at[h, c, far]
            send(blk, blk, d_s.at[h, 3], d_r.at[h, 3], mate)

    def ag6():
        for h in range(2):
            pp, qq = pos[h]
            for i, d in enumerate((0, -1, 1, 2)):
                blk = ad.at[h, 1 - c, (pp + d + 4) % 4]
                got(blk, d_s.at[h, i], d_r.at[h, i], mate)

    def zpart(s):
        for i in range(2):
            d = (z + NZ - 1 - s) % NZ if i == 0 else (z + 1 + s) % NZ
            fcol = pl.ds(pl.multiple_of(d * feat, feat), feat)

            def step(r, _):
                a = tok[pl.ds(pl.multiple_of(i * hrows + r * BLK, BLK), BLK), :]
                acc[i, pl.ds(pl.multiple_of(r * BLK, BLK), BLK), :] = jnp.dot(
                    a, w[:, fcol], preferred_element_type=F32
                )
                return 0

            lax.fori_loop(0, hrows // BLK, step, 0)

    def zsend(s):
        for u in range(SUB):
            for i in range(2):
                if s > 0:
                    got(zr.at[i, s - 1, u], z_s.at[i, s - 1, u], z_r.at[i, s - 1, u], zdev(1))

                def step(r, _):
                    rr = pl.ds(pl.multiple_of(r * BLK, BLK), BLK)
                    v = acc[i, pl.ds(pl.multiple_of(u * srows + r * BLK, BLK), BLK), :]
                    if s > 0:
                        v = v + zr[i, s - 1, u, rr, :].astype(F32)
                    zs[i, s, u, rr, :] = v.astype(BF)
                    return 0

                lax.fori_loop(0, srows // BLK, step, 0)
                send(
                    zs.at[i, s, u], zr.at[i, s, u], z_s.at[i, s, u], z_r.at[i, s, u],
                    zdev(1) if i == 0 else zdev(NZ - 1),
                )

    def zlast():
        last_step = NZ - 2
        for u in range(SUB):
            for i in range(2):
                got(zr.at[i, last_step, u], z_s.at[i, last_step, u], z_r.at[i, last_step, u], zdev(1))

                def step(r, _):
                    t = (i * hrows + u * srows) // TILE + r
                    k = adapter(t)
                    rr = pl.ds(pl.multiple_of(r * TILE, TILE), TILE)
                    v = acc[i, pl.ds(pl.multiple_of(u * srows + r * TILE, TILE), TILE), :]
                    v = v + zr[i, last_step, u, rr, :].astype(F32)
                    up = ad[k][:, width:]
                    l = low[t // 2, t % 2, pl.ds(0, rank), :]
                    upd = SCALE * lax.dot_general(l, up, (((0,), (0,)), ((), ())), preferred_element_type=F32)
                    v = v + upd.astype(BF).astype(F32)
                    val_o[pl.ds(pl.multiple_of(t * TILE, TILE), TILE), :] = v.astype(BF)
                    return 0

                lax.fori_loop(0, srows // TILE, step, 0)

    def adapter(t):
        a = ids[t]
        owner = a // OWN
        local = a % OWN
        h = local // 2
        cc = owner % 2
        xx = (owner // 2) % NX
        yy = owner // (2 * NX)
        pp = jnp.where(h == 0, yy, xx)
        qq = jnp.where(h == 0, xx, yy)
        return (h, cc, pp, qq, local % 2)

    def lowpart():
        def step(t, _):
            both = ad[adapter(t)]
            rr = pl.ds(pl.multiple_of(t * TILE, TILE), TILE)
            nt = (((1,), (1,)), ((), ()))
            lo = lax.dot_general(both[:, :width], tok[rr, :], nt, preferred_element_type=F32)
            gl = lax.dot_general(both[:, width:], cot[rr, :], nt, preferred_element_type=F32)
            part[t // 2, t % 2, pl.ds(0, rank), :] = lo.astype(BF)
            part[t // 2, t % 2, pl.ds(rank, rank), :] = gl.astype(BF)
            return 0

        lax.fori_loop(0, tiles, step, 0)

    def arsend():
        for d in range(1, NZ):
            to = (z + d) % NZ
            send(part.at[to], ar.at[d], ar_s.at[d], ar_r.at[d], zdev(d))

    def arsum():
        for d in range(1, NZ):
            got(ar.at[d], ar_s.at[d], ar_r.at[d], zdev(d))
        tot = part[z].astype(F32)
        for d in range(1, NZ):
            tot = tot + ar[d].astype(F32)
        low[z, :, pl.ds(0, rank), :] = tot[:, :rank].astype(BF)
        low[z, :, pl.ds(rank, rank), :] = (SCALE * tot[:, rank:]).astype(BF)
        for d in range(1, NZ):
            send(low.at[z], low.at[z], br_s.at[d], br_r.at[d], zdev(d))

    def argot():
        for d in range(1, NZ):
            got(low.at[(z + NZ - d) % NZ], br_s.at[d], br_r.at[d], zdev(d))

    def terms():
        def step(t, _):
            rr = pl.ds(pl.multiple_of(t * TILE, TILE), TILE)
            lo = low[t // 2, t % 2, pl.ds(0, rank), :]
            gl = low[t // 2, t % 2, pl.ds(rank, rank), :]
            tfull[t, :, pl.ds(0, width)] = jnp.dot(gl, tok[rr, :], preferred_element_type=F32).astype(BF)
            tfull[t, :, pl.ds(width, feat)] = (
                SCALE * jnp.dot(lo, cot[rr, :], preferred_element_type=F32)
            ).astype(BF)
            return 0

        lax.fori_loop(0, tiles, step, 0)

    mine = pl.ds(pl.multiple_of(c * half, 128), half)
    theirs = pl.ds(pl.multiple_of((1 - c) * half, 128), half)

    def tsend():
        send(
            tfull.at[pl.ds(0, tiles), :, theirs], tpart.at[pl.ds(0, tiles)], t_s.at[0], t_r.at[0], mate
        )

    def tables():
        cp = pltpu.make_async_copy(tab, tabs.at[0], lsem.at[7])
        cp.start()
        cp.wait()
        got(tabp, t_s.at[1], t_r.at[1], mate)
        cp = pltpu.make_async_copy(tabp, tabs.at[1], lsem.at[8])
        cp.start()
        cp.wait()

    def build(h, pp):
        def step(n, _):
            qq, cc, k = n // 4, (n // 2) % 2, n % 2
            yy, xx = (pp, qq) if h == 0 else (qq, pp)
            a = ((yy * NX + xx) * NC + cc) * OWN + 2 * h + k
            v = tfull[tabs[0, 0, a], :, mine].astype(F32) + tfull[tabs[0, 1, a], :, mine].astype(F32)
            v = v + tpart[tabs[1, 0, a]].astype(F32)
            v = v + tpart[tabs[1, 1, a]].astype(F32)
            g[h, pp, qq, cc, k] = v.astype(BF)
            return 0

        lax.fori_loop(0, 16, step, 0)

    def plus(h, i):
        return (pos[h][0] + 1) % 4 if i == 0 else (pos[h][0] + 3) % 4

    DIRS = ((0, 1), (1, -1))

    def rs1():
        for h in range(2):
            far = (pos[h][0] + 2) % 4
            build(h, far)
            for i, dp in DIRS:
                send(g.at[h, far, pl.ds(2 * i, 2)], r1.at[h, i], g_s.at[h, 0, i], g_r.at[h, 0, i], hdev(h, dp, 0))
        for h in range(2):
            for i, dp in DIRS:
                near = plus(h, i)
                build(h, near)
                raw = pl.ds(2 * (1 - i), 2)
                send(g.at[h, near, raw], r2.at[h, i, raw], g_s.at[h, 1, i], g_r.at[h, 1, i], hdev(h, dp, 0))

    def rs2():
        for h in range(2):
            for i, dp in DIRS:
                near = plus(h, i)
                got(r1.at[h, i], g_s.at[h, 0, i], g_r.at[h, 0, i], hdev(h, dp, 0))

                def step(n, _):
                    qq, cc = n // 2, n % 2
                    g[h, near, 2 * i + qq, cc] = (
                        g[h, near, 2 * i + qq, cc].astype(F32) + r1[h, i, qq, cc].astype(F32)
                    ).astype(BF)
                    return 0

                lax.fori_loop(0, 4, step, 0)
                summed = pl.ds(2 * i, 2)
                send(g.at[h, near, summed], r2.at[h, i, summed], g_s.at[h, 2, i], g_r.at[h, 2, i], hdev(h, dp, 0))

    def rs3():
        for h in range(2):
            build(h, pos[h][0])

    def rs4():
        for h in range(2):
            pp, qq0 = pos[h]
            for i, dp in DIRS:
                raw, summed = pl.ds(2 * (1 - i), 2), pl.ds(2 * i, 2)
                got(r2.at[h, i, raw], g_s.at[h, 1, i], g_r.at[h, 1, i], hdev(h, dp, 0))
                got(r2.at[h, i, summed], g_s.at[h, 2, i], g_r.at[h, 2, i], hdev(h, dp, 0))

            def step(n, _):
                qq, cc = n // 2, n % 2
                v = g[h, pp, qq, cc].astype(F32) + r2[h, 0, qq, cc].astype(F32) + r2[h, 1, qq, cc].astype(F32)
                sf[h, qq, cc] = v
                sb[h, qq, cc] = v.astype(BF)
                return 0

            lax.fori_loop(0, 8, step, 0)
            far = (qq0 + 2) % 4
            for i, dq in DIRS:
                near = (qq0 + dq + 4) % 4
                send(sb.at[h, far, i], r3.at[h, i], g_s.at[h, 3, i], g_r.at[h, 3, i], hdev(h, 0, dq))
                send(sb.at[h, near, 1 - i], r4.at[h, i, 1 - i], g_s.at[h, 4, i], g_r.at[h, 4, i], hdev(h, 0, dq))

    def rs5():
        for h in range(2):
            qq0 = pos[h][1]
            for i, dq in DIRS:
                near = (qq0 + dq + 4) % 4
                got(r3.at[h, i], g_s.at[h, 3, i], g_r.at[h, 3, i], hdev(h, 0, dq))
                sb[h, near, i] = (sf[h, near, i] + r3[h, i].astype(F32)).astype(BF)
                send(sb.at[h, near, i], r4.at[h, i, i], g_s.at[h, 5, i], g_r.at[h, 5, i], hdev(h, 0, dq))

    def rs6():
        for h in range(2):
            qq0 = pos[h][1]
            for i, dq in DIRS:
                got(r4.at[h, i, 1 - i], g_s.at[h, 4, i], g_r.at[h, 4, i], hdev(h, 0, dq))
                got(r4.at[h, i, i], g_s.at[h, 5, i], g_r.at[h, 5, i], hdev(h, 0, dq))
            for cc in range(2):
                fin[h, cc] = sf[h, qq0, cc] + r4[h, 0, cc].astype(F32) + r4[h, 1, cc].astype(F32)
            send(fin.at[h, 1 - c], rfin.at[h], f_s.at[h], f_r.at[h], mate)
            full[pl.ds(2 * h, 2), :, mine] = fin[h, c]
        for h in range(2):
            got(rfin.at[h], f_s.at[h], f_r.at[h], mate)
            full[pl.ds(2 * h, 2), :, theirs] = rfin[h]
        gd_o[...] = full[:, :, :width]
        ug_o[...] = full[:, :, width:]

    ag1()
    loads[4].wait()
    loads[5].wait()
    zpart(0)
    zsend(0)
    ag2()
    zpart(1)
    ag3()
    zsend(1)
    zpart(2)
    zsend(2)
    ag4()
    zpart(3)
    zsend(3)
    ag5()
    zpart(4)
    loads[6].wait()
    tables()
    ag6()
    lowpart()
    arsend()
    zsend(4)
    arsum()
    zpart(5)
    zsend(5)
    argot()
    terms()
    tsend()
    zpart(6)
    got(tpart.at[pl.ds(0, tiles)], t_s.at[0], t_r.at[0], mate)
    rs1()
    zsend(6)
    rs2()
    rs3()
    zpart(7)
    rs4()
    zlast()
    rs5()
    rs6()
    for cp in sent:
        cp.wait_send()


def body(tokens, value_weight, adapter_down_maps, adapter_up_maps, adapter_of_tile, cotangent):
    rows, width = tokens.shape
    feat = cotangent.shape[1]
    own, rank, _ = adapter_down_maps.shape
    tiles = rows // TILE
    cols = width + feat
    half = cols // 2
    hrows = rows // 2
    srows = hrows // SUB
    dma = pltpu.SemaphoreType.DMA
    vm = pltpu.VMEM
    any_spec = pl.BlockSpec(memory_space=pl.ANY)
    vmem = pl.BlockSpec(memory_space=pltpu.VMEM)
    return pl.pallas_call(
        kernel,
        out_shape=(
            jax.ShapeDtypeStruct((rows, feat), BF),
            jax.ShapeDtypeStruct((own, rank, width), F32),
            jax.ShapeDtypeStruct((own, rank, feat), F32),
        ),
        in_specs=[pl.BlockSpec(memory_space=pltpu.SMEM)] + [any_spec] * 5,
        out_specs=(vmem, vmem, vmem),
        scratch_shapes=[
            vm((rows, width), BF),
            vm(value_weight.shape, BF),
            vm((rows, feat), BF),
            vm((2, NC, 4, 4, 2, rank, cols), BF),
            vm((2, hrows, feat), F32),
            vm((2, NZ - 1, SUB, srows, feat), BF),
            vm((2, NZ - 1, SUB, srows, feat), BF),
            vm((NZ, tiles // NZ, 2 * rank, TILE), BF),
            vm((NZ, tiles // NZ, 2 * rank, TILE), BF),
            vm((NZ, tiles // NZ, 2 * rank, TILE), BF),
            vm((tiles + 1, rank, cols), BF),
            vm((tiles + 1, rank, half), BF),
            vm((8, 128), jnp.int32),
            vm((8, 128), jnp.int32),
            pltpu.SMEM((2, 8, 128), jnp.int32),
            vm((2, 4, 4, 2, 2, rank, half), BF),
            vm((2, 2, 2, 2, 2, rank, half), BF),
            vm((2, 2, 4, 2, 2, rank, half), BF),
            vm((2, 4, 2, 2, rank, half), F32),
            vm((2, 4, 2, 2, rank, half), BF),
            vm((2, 2, 2, rank, half), BF),
            vm((2, 2, 2, 2, rank, half), BF),
            vm((2, 2, 2, rank, half), F32),
            vm((2, 2, rank, half), F32),
            vm((own, rank, cols), F32),
            dma((9,)),
            dma((2, 4, 2)),
            dma((2, 4, 2)),
            dma((2, 4)),
            dma((2, 4)),
            dma((2, NZ - 1, SUB)),
            dma((2, NZ - 1, SUB)),
            dma((NZ,)),
            dma((NZ,)),
            dma((NZ,)),
            dma((NZ,)),
            dma((2,)),
            dma((2,)),
            dma((2, 6, 2)),
            dma((2, 6, 2)),
            dma((2,)),
            dma((2,)),
        ],
        compiler_params=pltpu.CompilerParams(
            collective_id=0, has_side_effects=True, vmem_limit_bytes=56 * 2**20
        ),
        name="adapters_and_projection",
    )(adapter_of_tile, tokens, value_weight, adapter_down_maps, adapter_up_maps, cotangent)


def solution(mesh):
    in_specs = (
        P("seq", "tensor"),
        P("tensor", None),
        P("seq", None, "tensor"),
        P("seq", None, "tensor"),
        P("seq"),
        P("seq", "tensor"),
    )
    out_specs = (P("seq", "tensor"), P("seq", None, "tensor"), P("seq", None, "tensor"))
    return jax.shard_map(body, mesh=mesh, in_specs=in_specs, out_specs=out_specs, check_vma=False)
```

time: 310 us -> 99.4 us (0.32)
  waiting for transfers between devices: 242 us -> 0 us
  Pallas kernels: 0 us -> 93.4 us
  other arithmetic: 19.8 us -> 0 us
  local copies, waits for them, and re-layouts: 21.2 us -> 5.06 us
  between operations: 13.8 us -> 0.64 us
  matrix products: 11.8 us -> 0 us
    pallas_call x0 -> x1, Pallas kernels: none -> 93.4 us  [body(): pl.pallas_call(kernel, out_shape=(jax.ShapeDtypeStruct((rows, feat), BF),...]
    reduce_scatter x1 -> x0, waiting for transfers between devices: 89.9 us -> none  [body(): lax.psum_scatter(summed.astype(jnp.bfloat16), 'seq', scatter_dimension=0,...]
    all_gather x1 -> x0, waiting for transfers between devices: 59.8 us -> none  [body(): all_adapters = lax.all_gather(adapters, 'seq', axis=0, tiled=True)]
    psum x1 -> x0, waiting for transfers between devices: 54.7 us -> none  [body(): sums = lax.psum(jnp.concatenate([low_part, glow_part], axis=1), 'tensor')]
    unnamed x5 -> x0, waiting for transfers between devices: 37.6 us -> none
    dot_general x6 -> x0, matrix products: 11.8 us -> none  [the longest x1 6.24 us: body(): lax.dot_general(tokens, value_weight, (((1,), (0,)), ((), ())), preferred...]
    convert_element_type x2 -> x0, other arithmetic: 10.5 us -> none  [the longest x1 8.54 us: body(): summed.astype(jnp.bfloat16)]
    broadcast_in_dim x1 -> x0, local copies, waits for them, and re-layouts: 6.14 us -> none  [body(): jnp.zeros((adapter_count,) + terms.shape[1:], jnp.float32)]
  transfers between devices with their start and end apart: 4 -> 0, of which waited for: 4 -> 0; matrix products, arithmetic and copies ran while one was open for 14% -> 0% of each run, Pallas kernels for 0% -> 0%
where the time goes in v2:
time: 99.4 us; the launch traced here: 99.1 us
  Pallas kernels  93.4 us (94%)
  local copies, waits for them, and re-layouts  5.06 us (5%)
    pallas_call x1, Pallas kernels, body(): pl.pallas_call(kernel, out_shape=(jax.ShapeDtypeStruct((rows, feat), BF),...  93.4 us
    unnamed x3, local copies, waits for them, and re-layouts  5.06 us

profile of v2, /device:TPU:1, one launch (start us, length us, event | category | flops | bytes accessed | tf_op | source)
XLA Modules:
  0.0 99.1 jit_solution(1880993858719923057)
XLA Ops:
  0.6 93.4 %adapters_and_projection.1 = (bf16[2048,128]{1,0:T(8,128)(2,1)}, f32[4,32,640]{2,1,0:T(8,128)}, f32[4,32,128]{2,1,0:T(8,128)}) custom-call(s32[16]{0:T(128)} %ids.1, bf16[2048,640]{1,0:T(8,128)(2,1)} %tok_h.1, bf16[640,1024]{1,0:T(8,128)(2,1)} %w_h.1, bf16[4,32,640]{2,1,0:T(8,128)(2,1)} %down_h.1, bf16[4,32,128]{2,1,0:T(8,128)(2,1)} %up_h.1, ...), custom_call_target="tpu_custom_call" | custom-call | tf_op jit(solution)/shard_map/adapters_and_projection/pallas_call | solution.py:443
  94.1 1.9 %copy.12 = bf16[2048,128]{1,0:T(8,128)(2,1)} copy(bf16[2048,128]{1,0:T(8,128)(2,1)} %get-tuple-element.6) | data formatting | bytes 1048576
  95.9 1.7 %copy.13 = f32[4,32,640]{2,1,0:T(8,128)} copy(f32[4,32,640]{2,1,0:T(8,128)} %get-tuple-element.7) | data formatting | bytes 655360
  97.7 1.5 %copy.14 = f32[4,32,128]{2,1,0:T(8,128)} copy(f32[4,32,128]{2,1,0:T(8,128)} %get-tuple-element.8) | data formatting | bytes 131072

commit v3 on v1

v3 whole, which is shorter than its diff:
```python
import jax
import jax.numpy as jnp
from jax import lax
from jax.experimental import pallas as pl
from jax.experimental.pallas import tpu as pltpu
from jax.sharding import PartitionSpec as P

TILE = 128
NX, NY, NC, NZ = 4, 4, 2, 8
OWN = 4
SCALE = 2.0
SUB = 2
BLK = 256
UN = 4
MESH = pl.DeviceIdType.MESH
BF = jnp.bfloat16
F32 = jnp.float32
DIRS = ((0, 1), (1, -1))
UP, DOWN = 0, 1
ALL_Q = ((0, 4),)
TWO_Q = ((0, 2), (2, 2))


def kernel(
    ids, tok_h, w_h, down_h, up_h, cot_h,
    val_o, gd_o, ug_o,
    tok, w, cot, adu, add, acc, zs, zr, part, ar, low, tu, td, tpu, tpd, tab, tabp, tabs, place_of,
    gu, gd, r1u, r1d, r2u, r2d, sfu, sfd, sbu, sbd, r3u, r3d, r4u, r4d, finu, find, rfu, rfd,
    lsem, ag_s, ag_r, d_s, d_r, z_s, z_r, ar_s, ar_r, br_s, br_r, t_s, t_r,
    g_s, g_r, q_s, q_r, f_s, f_r,
):
    width = tok.shape[1]
    rows = tok.shape[0]
    rank = down_h.shape[1]
    feat = cot.shape[1]
    tiles = rows // TILE
    hrank = rank // 2
    hrows = rows // 2
    srows = hrows // SUB
    ad = (adu, add)
    tt = (tu, td)
    tp = (tpu, tpd)
    g = (gu, gd)
    r1 = (r1u, r1d)
    r2 = (r2u, r2d)
    sf = (sfu, sfd)
    sb = (sbu, sbd)
    r3 = (r3u, r3d)
    r4 = (r4u, r4d)
    fin = (finu, find)
    rf = (rfu, rfd)
    out = (ug_o, gd_o)
    s_idx = lax.axis_index("seq")
    z = lax.axis_index("tensor")
    c = s_idx % 2
    x = (s_idx // 2) % NX
    y = s_idx // (2 * NX)
    pos = ((y, x), (x, y))

    def dev(yy, xx, cc):
        return ((yy * NX + xx) * NC + cc, z)

    def zdev(d):
        return (s_idx, (z + d) % NZ)

    def hdev(h, dp, dq):
        pp, qq = (pos[h][0] + dp + 4) % 4, (pos[h][1] + dq + 4) % 4
        return dev(pp, qq, c) if h == 0 else dev(qq, pp, c)

    mate = dev(y, x, 1 - c)

    def remote(src, dst, ss, rs, device):
        return pltpu.make_async_remote_copy(
            src_ref=src, dst_ref=dst, send_sem=ss, recv_sem=rs, device_id=device, device_id_type=MESH
        )

    sent = []

    def send(src, dst, ss, rs, device):
        cp = remote(src, dst, ss, rs, device)
        cp.start()
        sent.append(cp)

    def got(dst, ss, rs):
        remote(dst, dst, ss, rs, mate).wait_recv()

    def slot(h, side, p, q=0, k=0, n=1):
        return pl.ds((((h * 2 + side) * 4 + p) * 4 + q) * 2 + k, n)

    loads = []
    for h in range(2):
        loads.append(pltpu.make_async_copy(up_h.at[pl.ds(2 * h, 2)], adu.at[slot(h, 0, 0, n=2)], lsem.at[2 * h]))
        loads.append(pltpu.make_async_copy(down_h.at[pl.ds(2 * h, 2)], add.at[slot(h, 0, 0, n=2)], lsem.at[2 * h + 1]))
    loads.append(pltpu.make_async_copy(tok_h, tok, lsem.at[4]))
    loads.append(pltpu.make_async_copy(cot_h, cot, lsem.at[5]))
    for j in range(NZ + 1):
        d = (z + NZ - j) % NZ
        loads.append(
            pltpu.make_async_copy(
                w_h.at[:, pl.ds(pl.multiple_of(d * feat, feat), feat)],
                w.at[:, pl.ds(j * feat, feat)],
                lsem.at[8 + j],
            )
        )
    for cp in loads:
        cp.start()
    bar = pltpu.get_barrier_semaphore()
    friends = [zdev(d) for d in range(1, NZ)] + [mate]
    friends += [hdev(0, 1, 0), hdev(0, -1, 0), hdev(0, 0, 1), hdev(0, 0, -1)]
    for f in friends:
        pl.semaphore_signal(bar, inc=1, device_id=f, device_id_type=MESH)
    lane = lax.broadcasted_iota(jnp.int32, (8, 128), 1)
    lane_h = lane // 64
    lane_p = (lane // 16) % 4
    lane_q = (lane // 2) % 4
    lane_q = jnp.where(lane_q == 0, 2, jnp.where(lane_q == 1, 1, jnp.where(lane_q == 2, 3, 0)))
    lane_y = (y + jnp.where(lane_h == 0, lane_p, lane_q)) % 4
    lane_x = (x + jnp.where(lane_h == 0, lane_q, lane_p)) % 4
    lane_c = (lane // 8 + c) % 2
    named = ((lane_y * NX + lane_x) * NC + lane_c) * OWN + 2 * lane_h + lane % 2
    row = lax.broadcasted_iota(jnp.int32, (8, 128), 0)
    first = jnp.full((8, 128), tiles, jnp.int32)
    count = jnp.zeros((8, 128), jnp.int32)
    last = jnp.full((8, 128), tiles, jnp.int32)
    for t in range(tiles):
        hit = named == ids[t]
        last = jnp.where(hit & (count == 1), t, last)
        first = jnp.where(hit & (count == 0), t, first)
        count = count + hit.astype(jnp.int32)
    tab[...] = jnp.where(row == 0, first, last)
    for e in range(2):
        tt[e][tiles] = jnp.zeros(tt[e].shape[1:], BF)
        tp[e][tiles] = jnp.zeros(tp[e].shape[1:], BF)
    for t in range(tiles):
        a = ids[t]
        owner = a // OWN
        h = (a % OWN) // 2
        xx = (owner // 2 + NX - x) % NX
        yy = (owner // (2 * NX) + NY - y) % NY
        pq = jnp.where(h == 0, yy * 4 + xx, xx * 4 + yy)
        place_of[t] = ((h * 2 + (owner + c) % 2) * 16 + pq) * 2 + a % 2
    for cp in loads[:4]:
        cp.wait()
    pl.semaphore_wait(bar, len(friends))

    def ag1(e):
        for h in range(2):
            own = ad[e].at[slot(h, 0, 0, n=2)]
            for i, dq in DIRS:
                send(own, ad[e].at[slot(h, 0, 0, 3 - 2 * i, n=2)], ag_s.at[e, h, 0, i], ag_r.at[e, h, 0, i], hdev(h, 0, dq))

    def ag1p(e):
        for h in range(2):
            own = ad[e].at[slot(h, 0, 0, n=2)]
            for i, dp in DIRS:
                send(own, ad[e].at[slot(h, 0, 3 - 2 * i, n=2)], ag_s.at[e, h, 4, i], ag_r.at[e, h, 4, i], hdev(h, dp, 0))

    def ag2(e):
        for h in range(2):
            for i, dq in DIRS:
                near = 3 - 2 * i
                got(ad[e].at[slot(h, 0, 0, near, n=2)], ag_s.at[e, h, 0, i], ag_r.at[e, h, 0, i])
                send(
                    ad[e].at[slot(h, 0, 0, near, i)], ad[e].at[slot(h, 0, 0, 2, i)],
                    ag_s.at[e, h, 1, i], ag_r.at[e, h, 1, i], hdev(h, 0, dq),
                )

    def ag3(e):
        for h in range(2):
            for i, dq in DIRS:
                got(ad[e].at[slot(h, 0, 0, 2, i)], ag_s.at[e, h, 1, i], ag_r.at[e, h, 1, i])
            for i, dp in DIRS:
                send(
                    ad[e].at[slot(h, 0, 0, 1, n=6)], ad[e].at[slot(h, 0, 3 - 2 * i, 1, n=6)],
                    ag_s.at[e, h, 2, i], ag_r.at[e, h, 2, i], hdev(h, dp, 0),
                )
            send(ad[e].at[slot(h, 0, 0, n=8)], ad[e].at[slot(h, 1, 0, n=8)], d_s.at[e, h, 0], d_r.at[e, h, 0], mate)

    def ag4(e):
        for h in range(2):
            for i, dp in DIRS:
                near = 3 - 2 * i
                got(ad[e].at[slot(h, 0, near, n=2)], ag_s.at[e, h, 4, i], ag_r.at[e, h, 4, i])
                got(ad[e].at[slot(h, 0, near, 1, n=6)], ag_s.at[e, h, 2, i], ag_r.at[e, h, 2, i])
                send(
                    ad[e].at[slot(h, 0, near, 2 * i, n=4)], ad[e].at[slot(h, 0, 2, 2 * i, n=4)],
                    ag_s.at[e, h, 3, i], ag_r.at[e, h, 3, i], hdev(h, dp, 0),
                )
                send(ad[e].at[slot(h, 0, near, n=8)], ad[e].at[slot(h, 1, near, n=8)], d_s.at[e, h, near], d_r.at[e, h, near], mate)

    def ag5(e):
        for h in range(2):
            for i, dp in DIRS:
                got(ad[e].at[slot(h, 0, 2, 2 * i, n=4)], ag_s.at[e, h, 3, i], ag_r.at[e, h, 3, i])
            send(ad[e].at[slot(h, 0, 2, n=8)], ad[e].at[slot(h, 1, 2, n=8)], d_s.at[e, h, 2], d_r.at[e, h, 2], mate)

    def ag6(e):
        for h in range(2):
            for j in range(4):
                got(ad[e].at[slot(h, 1, j, n=8)], d_s.at[e, h, j], d_r.at[e, h, j])

    def zpart(m):
        for i in range(2):
            start = (2 * m + 1) * feat if i == 0 else (6 - 2 * m) * feat

            def step(r, _):
                rr = pl.ds(pl.multiple_of(r * BLK, BLK), BLK)
                a = tok[pl.ds(pl.multiple_of(i * hrows + r * BLK, BLK), BLK), :]
                v = jnp.dot(a, w[:, start : start + 2 * feat], preferred_element_type=F32)
                acc[m % 2, i, i, rr, :] = v[:, :feat]
                acc[m % 2, i, 1 - i, rr, :] = v[:, feat:]
                return 0

            lax.fori_loop(0, hrows // BLK, step, 0)

    def zsend(s, u):
        for i in range(2):
            if s > 0:
                got(zr.at[i, s - 1, u], z_s.at[i, s - 1, u], z_r.at[i, s - 1, u])

            def step(r, _):
                rr = pl.ds(pl.multiple_of(r * 128, 128), 128)
                v = acc[(s // 2) % 2, i, s % 2, pl.ds(pl.multiple_of(u * srows + r * 128, 128), 128), :]
                if s > 0:
                    v = v + zr[i, s - 1, u, rr, :].astype(F32)
                zs[i, s, u, rr, :] = v.astype(BF)
                return 0

            lax.fori_loop(0, srows // 128, step, 0)
            send(
                zs.at[i, s, u], zr.at[i, s, u], z_s.at[i, s, u], z_r.at[i, s, u],
                zdev(1) if i == 0 else zdev(NZ - 1),
            )

    def zlast():
        last_step = NZ - 2
        for u in range(SUB):
            for i in range(2):
                got(zr.at[i, last_step, u], z_s.at[i, last_step, u], z_r.at[i, last_step, u])

                def step(r, _):
                    t = (i * hrows + u * srows) // TILE + r
                    rr = pl.ds(pl.multiple_of(r * TILE, TILE), TILE)
                    v = acc[1, i, 1, pl.ds(pl.multiple_of(u * srows + r * TILE, TILE), TILE), :]
                    v = v + zr[i, last_step, u, rr, :].astype(F32)
                    upd = SCALE * lax.dot_general(
                        low[DOWN, t // 2, t % 2], adu[place_of[t]], (((0,), (0,)), ((), ())),
                        preferred_element_type=F32,
                    )
                    v = v + upd.astype(BF).astype(F32)
                    val_o[pl.ds(pl.multiple_of(t * TILE, TILE), TILE), :] = v.astype(BF)
                    return 0

                lax.fori_loop(0, srows // TILE, step, 0, unroll=UN)

    def lowpart(e):
        source = (cot, tok)[e]

        def step(t, _):
            rr = pl.ds(pl.multiple_of(t * TILE, TILE), TILE)
            v = lax.dot_general(
                ad[e][place_of[t]], source[rr, :], (((1,), (1,)), ((), ())), preferred_element_type=F32
            )
            part[e, t // 2, t % 2] = v.astype(BF)
            return 0

        lax.fori_loop(0, tiles, step, 0, unroll=UN)

    ORDER = (4, 3, 5, 2, 6, 1, 7)

    def arsend(e):
        lowpart(e)
        for d in ORDER:
            send(part.at[e, (z + d) % NZ], ar.at[e, d], ar_s.at[e, d], ar_r.at[e, d], zdev(d))

    def arsum(e):
        for d in range(1, NZ):
            got(ar.at[e, d], ar_s.at[e, d], ar_r.at[e, d])
        tot = part[e, z].astype(F32)
        for d in range(1, NZ):
            tot = tot + ar[e, d].astype(F32)
        if e == UP:
            tot = SCALE * tot
        low[e, z] = tot.astype(BF)
        for d in ORDER:
            send(low.at[e, z], low.at[e, z], br_s.at[e, d], br_r.at[e, d], zdev(d))

    def argot(e):
        for d in range(1, NZ):
            got(low.at[e, (z + NZ - d) % NZ], br_s.at[e, d], br_r.at[e, d])

    mine = pl.ds(pl.multiple_of(c * hrank, hrank), hrank)
    theirs = pl.ds(pl.multiple_of((1 - c) * hrank, hrank), hrank)

    def terms(e):
        source = (cot, tok)[e]

        def step(t, _):
            rr = pl.ds(pl.multiple_of(t * TILE, TILE), TILE)
            v = jnp.dot(low[1 - e, t // 2, t % 2], source[rr, :], preferred_element_type=F32)
            if e == UP:
                v = SCALE * v
            tt[e][t] = v.astype(BF)
            return 0

        lax.fori_loop(0, tiles, step, 0, unroll=UN)
        send(tt[e].at[pl.ds(0, tiles), theirs, :], tp[e].at[pl.ds(0, tiles)], t_s.at[e], t_r.at[e], mate)

    def tgot(e):
        got(tp[e].at[pl.ds(0, tiles)], t_s.at[e], t_r.at[e])

    def tables():
        cp = pltpu.make_async_copy(tab, tabs.at[0], lsem.at[6])
        cp.start()
        cp.wait()
        got(tabp, t_s.at[2], t_r.at[2])
        cp = pltpu.make_async_copy(tabp, tabs.at[1], lsem.at[7])
        cp.start()
        cp.wait()

    def build(e, h, rel, group):
        q0, n = group
        base = (h * 4 + rel) * 16
        for cc in range(2):
            here = base + cc * 8 + 2 * q0
            there = base + (1 - cc) * 8 + 2 * q0

            def step(j, _):
                v = tt[e][tabs[0, 0, here + j], mine, :].astype(F32)
                v = v + tt[e][tabs[0, 1, here + j], mine, :].astype(F32)
                v = v + tp[e][tabs[1, 0, there + j]].astype(F32)
                v = v + tp[e][tabs[1, 1, there + j]].astype(F32)
                g[e][h, rel, cc, 2 * q0 + j] = v.astype(BF)
                return 0

            lax.fori_loop(0, 2 * n, step, 0, unroll=min(UN, 2 * n))

    NEAR = (1, 3)

    def rs1far(e, groups, gi):
        q0, n = groups[gi]
        qs = pl.ds(2 * q0, 2 * n)
        for h in range(2):
            build(e, h, 2, groups[gi])
            for i, dp in DIRS:
                send(
                    g[e].at[h, 2, i, qs], r1[e].at[h, i, qs],
                    g_s.at[e, h, gi, 0, i], g_r.at[e, h, gi, 0, i], hdev(h, dp, 0),
                )

    def rs1near(e, groups, gi):
        q0, n = groups[gi]
        qs = pl.ds(2 * q0, 2 * n)
        for h in range(2):
            for i, dp in DIRS:
                build(e, h, NEAR[i], groups[gi])
                send(
                    g[e].at[h, NEAR[i], 1 - i, qs], r2[e].at[h, i, 1 - i, qs],
                    g_s.at[e, h, gi, 1, i], g_r.at[e, h, gi, 1, i], hdev(h, dp, 0),
                )

    def rs2(e, groups, gi):
        q0, n = groups[gi]
        qs = pl.ds(2 * q0, 2 * n)
        for h in range(2):
            for i, dp in DIRS:
                got(r1[e].at[h, i, qs], g_s.at[e, h, gi, 0, i], g_r.at[e, h, gi, 0, i])

                def step(j, _):
                    v = g[e][h, NEAR[i], i, 2 * q0 + j].astype(F32) + r1[e][h, i, 2 * q0 + j].astype(F32)
                    g[e][h, NEAR[i], i, 2 * q0 + j] = v.astype(BF)
                    return 0

                lax.fori_loop(0, 2 * n, step, 0, unroll=UN)
                send(
                    g[e].at[h, NEAR[i], i, qs], r2[e].at[h, i, i, qs],
                    g_s.at[e, h, gi, 2, i], g_r.at[e, h, gi, 2, i], hdev(h, dp, 0),
                )

    def rs3(e):
        for h in range(2):
            build(e, h, 0, (0, 4))

    def rs4(e, groups, gi):
        q0, n = groups[gi]
        qs = pl.ds(2 * q0, 2 * n)
        for h in range(2):
            for i, dp in DIRS:
                got(r2[e].at[h, i, 1 - i, qs], g_s.at[e, h, gi, 1, i], g_r.at[e, h, gi, 1, i])
                got(r2[e].at[h, i, i, qs], g_s.at[e, h, gi, 2, i], g_r.at[e, h, gi, 2, i])
            for cc in range(2):

                def step(j, _):
                    qk = 2 * q0 + j
                    v = g[e][h, 0, cc, qk].astype(F32) + r2[e][h, 0, cc, qk].astype(F32)
                    v = v + r2[e][h, 1, cc, qk].astype(F32)
                    sf[e][h, cc, qk] = v
                    sb[e][h, cc, qk] = v.astype(BF)
                    return 0

                lax.fori_loop(0, 2 * n, step, 0, unroll=UN)
            for i, dq in DIRS:
                if q0 == 0:
                    send(
                        sb[e].at[h, i, pl.ds(0, 2)], r3[e].at[h, i],
                        q_s.at[e, h, 0, i], q_r.at[e, h, 0, i], hdev(h, 0, dq),
                    )
                if q0 <= 1 + i < q0 + n:
                    send(
                        sb[e].at[h, 1 - i, pl.ds(2 + 2 * i, 2)], r4[e].at[h, i, 1 - i],
                        q_s.at[e, h, 1, i], q_r.at[e, h, 1, i], hdev(h, 0, dq),
                    )

    def rs5(e):
        for h in range(2):
            for i, dq in DIRS:
                got(r3[e].at[h, i], q_s.at[e, h, 0, i], q_r.at[e, h, 0, i])
                unit = pl.ds(2 + 2 * i, 2)
                sb[e][h, i, unit] = (sf[e][h, i, unit] + r3[e][h, i].astype(F32)).astype(BF)
                send(
                    sb[e].at[h, i, unit], r4[e].at[h, i, i],
                    q_s.at[e, h, 2, i], q_r.at[e, h, 2, i], hdev(h, 0, dq),
                )

    def rs6(e):
        for h in range(2):
            for i, dq in DIRS:
                got(r4[e].at[h, i, 1 - i], q_s.at[e, h, 1, i], q_r.at[e, h, 1, i])
                got(r4[e].at[h, i, i], q_s.at[e, h, 2, i], q_r.at[e, h, 2, i])
            own = pl.ds(6, 2)
            fin[e][h] = sf[e][h, 1, own] + r4[e][h, 0, 1].astype(F32) + r4[e][h, 1, 1].astype(F32)
            send(fin[e].at[h], rf[e].at[h], f_s.at[e, h], f_r.at[e, h], mate)
            v = sf[e][h, 0, own] + r4[e][h, 0, 0].astype(F32) + r4[e][h, 1, 0].astype(F32)
            out[e][pl.ds(2 * h, 2), mine, :] = v

    def rs7(e):
        for h in range(2):
            got(rf[e].at[h], f_s.at[e, h], f_r.at[e, h])
            out[e][pl.ds(2 * h, 2), theirs, :] = rf[e][h]

    def tabsend():
        send(tab, tabp, t_s.at[2], t_r.at[2], mate)

    def landed(*which):
        for j in which:
            for cp in loads[j:] if j == 6 else loads[j : j + 1]:
                cp.wait()

    plan = (
        (ag1, UP),
        (ag1p, UP),
        (tabsend,),
        (landed, 4, 6),
        (zpart, 0),
        (zsend, 0, 0),
        (zsend, 0, 1),
        (ag2, UP),
        (ag1, DOWN),
        (landed, 5),
        (tables,),
        (ag3, UP),
        (ag1p, DOWN),
        (ag4, UP),
        (zsend, 1, 0),
        (ag2, DOWN),
        (zsend, 1, 1),
        (ag5, UP),
        (ag3, DOWN),
        (zpart, 1),
        (ag6, UP),
        (arsend, UP),
        (zsend, 2, 0),
        (zsend, 2, 1),
        (ag4, DOWN),
        (arsum, UP),
        (zsend, 3, 0),
        (zpart, 2),
        (zsend, 3, 1),
        (argot, UP),
        (terms, DOWN),
        (ag5, DOWN),
        (zsend, 4, 0),
        (tgot, DOWN),
        (rs1far, DOWN, TWO_Q, 0),
        (zsend, 4, 1),
        (ag6, DOWN),
        (arsend, DOWN),
        (rs1far, DOWN, TWO_Q, 1),
        (rs1near, DOWN, TWO_Q, 0),
        (zsend, 5, 0),
        (rs1near, DOWN, TWO_Q, 1),
        (zsend, 5, 1),
        (arsum, DOWN),
        (zpart, 3),
        (rs2, DOWN, TWO_Q, 0),
        (rs2, DOWN, TWO_Q, 1),
        (zsend, 6, 0),
        (zsend, 6, 1),
        (rs3, DOWN),
        (argot, DOWN),
        (terms, UP),
        (rs4, DOWN, TWO_Q, 0),
        (tgot, UP),
        (rs1far, UP, ALL_Q, 0),
        (rs1near, UP, ALL_Q, 0),
        (rs4, DOWN, TWO_Q, 1),
        (rs3, UP),
        (rs2, UP, ALL_Q, 0),
        (rs5, DOWN),
        (zlast,),
        (rs4, UP, ALL_Q, 0),
        (rs6, DOWN),
        (rs5, UP),
        (rs7, DOWN),
        (rs6, UP),
        (rs7, UP),
    )
    for act, *details in plan:
        act(*details)
    for cp in sent:
        cp.wait_send()


def place(val_i, gd_i, ug_i, val_o, gd_o, ug_o):
    val_o[...] = val_i[...]
    gd_o[...] = gd_i[...]
    ug_o[...] = ug_i[...]


def body(tokens, value_weight, adapter_down_maps, adapter_up_maps, adapter_of_tile, cotangent):
    rows, width = tokens.shape
    feat = cotangent.shape[1]
    own, rank, _ = adapter_down_maps.shape
    tiles = rows // TILE
    hrank = rank // 2
    hrows = rows // 2
    srows = hrows // SUB
    dma = pltpu.SemaphoreType.DMA
    vm = pltpu.VMEM
    any_spec = pl.BlockSpec(memory_space=pl.ANY)
    vmem = pl.BlockSpec(memory_space=pltpu.VMEM)
    both = (feat, width)
    shapes = (
        jax.ShapeDtypeStruct((rows, feat), BF),
        jax.ShapeDtypeStruct((own, rank, width), F32),
        jax.ShapeDtypeStruct((own, rank, feat), F32),
    )

    def pair(dims, lead, kind):
        return [vm(lead + (dims, n), kind) for n in both]

    results = pl.pallas_call(
        kernel,
        out_shape=shapes,
        in_specs=[pl.BlockSpec(memory_space=pltpu.SMEM)] + [any_spec] * 5,
        out_specs=(vmem, vmem, vmem),
        scratch_shapes=[
            vm((rows, width), BF),
            vm((width, (NZ + 1) * feat), BF),
            vm((rows, feat), BF),
            *pair(rank, (2 * NC * 4 * 4 * 2,), BF),
            vm((2, 2, 2, hrows, feat), F32),
            vm((2, NZ - 1, SUB, srows, feat), BF),
            vm((2, NZ - 1, SUB, srows, feat), BF),
            vm((2, NZ, tiles // NZ, rank, TILE), BF),
            vm((2, NZ, tiles // NZ, rank, TILE), BF),
            vm((2, NZ, tiles // NZ, rank, TILE), BF),
            *pair(rank, (tiles + 1,), BF),
            *pair(hrank, (tiles + 1,), BF),
            vm((8, 128), jnp.int32),
            vm((8, 128), jnp.int32),
            pltpu.SMEM((2, 8, 128), jnp.int32),
            pltpu.SMEM((tiles,), jnp.int32),
            *pair(hrank, (2, 4, 2, 8), BF),
            *pair(hrank, (2, 2, 8), BF),
            *pair(hrank, (2, 2, 2, 8), BF),
            *pair(hrank, (2, 2, 8), F32),
            *pair(hrank, (2, 2, 8), BF),
            *pair(hrank, (2, 2, 2), BF),
            *pair(hrank, (2, 2, 2, 2), BF),
            *pair(hrank, (2, 2), F32),
            *pair(hrank, (2, 2), F32),
            dma((8 + NZ + 1,)),
            dma((2, 2, 5, 2)),
            dma((2, 2, 5, 2)),
            dma((2, 2, 4)),
            dma((2, 2, 4)),
            dma((2, NZ - 1, SUB)),
            dma((2, NZ - 1, SUB)),
            dma((2, NZ)),
            dma((2, NZ)),
            dma((2, NZ)),
            dma((2, NZ)),
            dma((3,)),
            dma((3,)),
            dma((2, 2, 2, 3, 2)),
            dma((2, 2, 2, 3, 2)),
            dma((2, 2, 3, 2)),
            dma((2, 2, 3, 2)),
            dma((2, 2)),
            dma((2, 2)),
        ],
        compiler_params=pltpu.CompilerParams(
            collective_id=0, has_side_effects=True, vmem_limit_bytes=56 * 2**20
        ),
        name="adapters_and_projection",
    )(adapter_of_tile, tokens, value_weight, adapter_down_maps, adapter_up_maps, cotangent)
    return pl.pallas_call(
        place,
        out_shape=shapes,
        in_specs=[vmem] * 3,
        out_specs=(vmem,) * 3,
        name="place_results",
    )(*results)


def solution(mesh):
    in_specs = (
        P("seq", "tensor"),
        P("tensor", None),
        P("seq", None, "tensor"),
        P("seq", None, "tensor"),
        P("seq"),
        P("seq", "tensor"),
    )
    out_specs = (P("seq", "tensor"), P("seq", None, "tensor"), P("seq", None, "tensor"))
    return jax.shard_map(body, mesh=mesh, in_specs=in_specs, out_specs=out_specs, check_vma=False)
```

time: 310 us -> 89.9 us (0.29)
  waiting for transfers between devices: 242 us -> 0 us
  Pallas kernels: 0 us -> 89.1 us
  local copies, waits for them, and re-layouts: 21.2 us -> 0 us
  other arithmetic: 19.8 us -> 0 us
  between operations: 13.8 us -> 0.64 us
  matrix products: 11.8 us -> 0 us
    reduce_scatter x1 -> x0, waiting for transfers between devices: 89.9 us -> none  [body(): lax.psum_scatter(summed.astype(jnp.bfloat16), 'seq', scatter_dimension=0,...]
    pallas_call x0 -> x2, Pallas kernels: none -> 89.1 us  [the longest x1 87 us: body(): pl.pallas_call(kernel, out_shape=shapes, in_specs=[pl.BlockSpec(memory_sp...]
    all_gather x1 -> x0, waiting for transfers between devices: 59.8 us -> none  [body(): all_adapters = lax.all_gather(adapters, 'seq', axis=0, tiled=True)]
    psum x1 -> x0, waiting for transfers between devices: 54.7 us -> none  [body(): sums = lax.psum(jnp.concatenate([low_part, glow_part], axis=1), 'tensor')]
    unnamed x5 -> x0, waiting for transfers between devices: 37.6 us -> none
    dot_general x6 -> x0, matrix products: 11.8 us -> none  [the longest x1 6.24 us: body(): lax.dot_general(tokens, value_weight, (((1,), (0,)), ((), ())), preferred...]
    convert_element_type x2 -> x0, other arithmetic: 10.5 us -> none  [the longest x1 8.54 us: body(): summed.astype(jnp.bfloat16)]
    unnamed x6 -> x0, local copies, waits for them, and re-layouts: 8.59 us -> none
  transfers between devices with their start and end apart: 4 -> 0, of which waited for: 4 -> 0; matrix products, arithmetic and copies ran while one was open for 14% -> 0% of each run, Pallas kernels for 0% -> 0%
where the time goes in v3:
time: 89.9 us; the launch traced here: 89.7 us
  Pallas kernels  89.1 us (99%)
    pallas_call x1, Pallas kernels, body(): pl.pallas_call(kernel, out_shape=shapes, in_specs=[pl.BlockSpec(memory_sp...  87 us
    pallas_call x1, Pallas kernels, body(): pl.pallas_call(place, out_shape=shapes, in_specs=[vmem] * 3, out_specs=(v...  2.08 us

profile of v3, /device:TPU:1, one launch (start us, length us, event | category | flops | bytes accessed | tf_op | source)
XLA Modules:
  0.0 89.7 jit_solution(1569237524625294446)
XLA Ops:
  0.6 87.0 %adapters_and_projection.1 = (bf16[2048,128]{1,0:T(8,128)(2,1)}, f32[4,32,640]{2,1,0:T(8,128)}, f32[4,32,128]{2,1,0:T(8,128)}) custom-call(s32[16]{0:T(128)} %ids.1, bf16[2048,640]{1,0:T(8,128)(2,1)} %tok_h.1, bf16[640,1024]{1,0:T(8,128)(2,1)} %w_h.1, bf16[4,32,640]{2,1,0:T(8,128)(2,1)} %down_h.1, bf16[4,32,128]{2,1,0:T(8,128)(2,1)} %up_h.1, ...), custom_call_target="tpu_custom_call" | custom-call | tf_op jit(solution)/shard_map/adapters_and_projection/pallas_call | solution.py:552
  87.7 2.1 %place_results.1 = (bf16[2048,128]{1,0:T(8,128)(2,1)}, f32[4,32,640]{2,1,0:T(8,128)}, f32[4,32,128]{2,1,0:T(8,128)}) custom-call(bf16[2048,128]{1,0:T(8,128)(2,1)} %get-tuple-element.6.val_i, f32[4,32,640]{2,1,0:T(8,128)} %get-tuple-element.7.gd_i, f32[4,32,128]{2,1,0:T(8,128)} %get-tuple-element.8.ug_i), custom_call_target="tpu_custom_call" | custom-call | tf_op jit(solution)/shard_map/place_results/pallas_call | solution.py:608

commit v4 on v3

--- a/solution.py
+++ b/solution.py
@@ -25,7 +25,7 @@
     ids, tok_h, w_h, down_h, up_h, cot_h,
     val_o, gd_o, ug_o,
     tok, w, cot, adu, add, acc, zs, zr, part, ar, low, tu, td, tpu, tpd, tab, tabp, tabs, place_of,
-    gu, gd, r1u, r1d, r2u, r2d, sfu, sfd, sbu, sbd, r3u, r3d, r4u, r4d, finu, find, rfu, rfd,
+    gu, gd, r1u, r1d, r2d, sfu, sfd, sbu, sbd, r3u, r3d, r4d, finu, find, rfu, rfd,
     lsem, ag_s, ag_r, d_s, d_r, z_s, z_r, ar_s, ar_r, br_s, br_r, t_s, t_r,
     g_s, g_r, q_s, q_r, f_s, f_r,
 ):
@@ -42,11 +42,11 @@
     tp = (tpu, tpd)
     g = (gu, gd)
     r1 = (r1u, r1d)
-    r2 = (r2u, r2d)
+    r2 = (None, r2d)
     sf = (sfu, sfd)
     sb = (sbu, sbd)
     r3 = (r3u, r3d)
-    r4 = (r4u, r4d)
+    r4 = (None, r4d)
     fin = (finu, find)
     rf = (rfu, rfd)
     out = (ug_o, gd_o)
@@ -106,7 +106,7 @@
         cp.start()
     bar = pltpu.get_barrier_semaphore()
     friends = [zdev(d) for d in range(1, NZ)] + [mate]
-    friends += [hdev(0, 1, 0), hdev(0, -1, 0), hdev(0, 0, 1), hdev(0, 0, -1)]
+    friends += [hdev(0, d, 0) for d in (1, 2, 3)] + [hdev(0, 0, d) for d in (1, 2, 3)]
     for f in friends:
         pl.semaphore_signal(bar, inc=1, device_id=f, device_id_type=MESH)
     lane = lax.broadcasted_iota(jnp.int32, (8, 128), 1)
@@ -143,6 +143,36 @@
         cp.wait()
     pl.semaphore_wait(bar, len(friends))
 
+    def upq():
+        for h in range(2):
+            own = adu.at[slot(h, 0, 0, n=2)]
+            for d in (1, 3, 2):
+                send(
+                    own, adu.at[slot(h, 0, 0, 4 - d, n=2)],
+                    ag_s.at[UP, h, d, 0], ag_r.at[UP, h, d, 0], hdev(h, 0, d),
+                )
+
+    def upp():
+        for h in range(2):
+            for d in (1, 3, 2):
+                got(adu.at[slot(h, 0, 0, 4 - d, n=2)], ag_s.at[UP, h, d, 0], ag_r.at[UP, h, d, 0])
+            for d in (2, 1, 3):
+                send(
+                    adu.at[slot(h, 0, 0, n=8)], adu.at[slot(h, 0, 4 - d, n=8)],
+                    ag_s.at[UP, h, d, 1], ag_r.at[UP, h, d, 1], hdev(h, d, 0),
+                )
+        for h in range(2):
+            send(adu.at[slot(h, 0, 0, n=8)], adu.at[slot(h, 1, 0, n=8)], d_s.at[UP, h, 0], d_r.at[UP, h, 0], mate)
+
+    def upd():
+        for d in (1, 3, 2):
+            for h in range(2):
+                got(adu.at[slot(h, 0, 4 - d, n=8)], ag_s.at[UP, h, d, 1], ag_r.at[UP, h, d, 1])
+                send(
+                    adu.at[slot(h, 0, 4 - d, n=8)], adu.at[slot(h, 1, 4 - d, n=8)],
+                    d_s.at[UP, h, 4 - d], d_r.at[UP, h, 4 - d], mate,
+                )
+
     def ag1(e):
         for h in range(2):
             own = ad[e].at[slot(h, 0, 0, n=2)]
@@ -232,26 +262,25 @@
                 zdev(1) if i == 0 else zdev(NZ - 1),
             )
 
-    def zlast():
+    def zlast(u):
         last_step = NZ - 2
-        for u in range(SUB):
-            for i in range(2):
-                got(zr.at[i, last_step, u], z_s.at[i, last_step, u], z_r.at[i, last_step, u])
-
-                def step(r, _):
-                    t = (i * hrows + u * srows) // TILE + r
-                    rr = pl.ds(pl.multiple_of(r * TILE, TILE), TILE)
-                    v = acc[1, i, 1, pl.ds(pl.multiple_of(u * srows + r * TILE, TILE), TILE), :]
-                    v = v + zr[i, last_step, u, rr, :].astype(F32)
-                    upd = SCALE * lax.dot_general(
-                        low[DOWN, t // 2, t % 2], adu[place_of[t]], (((0,), (0,)), ((), ())),
-                        preferred_element_type=F32,
-                    )
-                    v = v + upd.astype(BF).astype(F32)
-                    val_o[pl.ds(pl.multiple_of(t * TILE, TILE), TILE), :] = v.astype(BF)
-                    return 0
-
-                lax.fori_loop(0, srows // TILE, step, 0, unroll=UN)
+        for i in range(2):
+            got(zr.at[i, last_step, u], z_s.at[i, last_step, u], z_r.at[i, last_step, u])
+
+            def step(r, _):
+                t = (i * hrows + u * srows) // TILE + r
+                rr = pl.ds(pl.multiple_of(r * TILE, TILE), TILE)
+                v = acc[1, i, 1, pl.ds(pl.multiple_of(u * srows + r * TILE, TILE), TILE), :]
+                v = v + zr[i, last_step, u, rr, :].astype(F32)
+                upd = SCALE * lax.dot_general(
+                    low[DOWN, t // 2, t % 2], adu[place_of[t]], (((0,), (0,)), ((), ())),
+                    preferred_element_type=F32,
+                )
+                v = v + upd.astype(BF).astype(F32)
+                val_o[pl.ds(pl.multiple_of(t * TILE, TILE), TILE), :] = v.astype(BF)
+                return 0
+
+            lax.fori_loop(0, srows // TILE, step, 0, unroll=UN)
 
     def lowpart(e):
         source = (cot, tok)[e]
@@ -438,6 +467,52 @@
             got(rf[e].at[h], f_s.at[e, h], f_r.at[e, h])
             out[e][pl.ds(2 * h, 2), theirs, :] = rf[e][h]
 
+    def us1():
+        for h in range(2):
+            for d in (2, 1, 3):
+                build(UP, h, d, (0, 4))
+                send(
+                    gu.at[h, d], r1u.at[h, d - 1],
+                    g_s.at[UP, h, 0, d - 1, 0], g_r.at[UP, h, 0, d - 1, 0], hdev(h, d, 0),
+                )
+        for h in range(2):
+            build(UP, h, 0, (0, 4))
+
+    def us2():
+        for h in range(2):
+            for d in (1, 3, 2):
+                got(r1u.at[h, d - 1], g_s.at[UP, h, 0, d - 1, 0], g_r.at[UP, h, 0, d - 1, 0])
+            for cc in range(2):
+
+                def step(j, _):
+                    v = gu[h, 0, cc, j].astype(F32) + r1u[h, 0, cc, j].astype(F32)
+                    v = v + r1u[h, 1, cc, j].astype(F32) + r1u[h, 2, cc, j].astype(F32)
+                    sfu[h, cc, j] = v
+                    sbu[h, cc, j] = v.astype(BF)
+                    return 0
+
+                lax.fori_loop(0, 8, step, 0, unroll=UN)
+            for qi, d in enumerate((2, 1, 3)):
+                send(
+                    sbu.at[h, :, pl.ds(2 * qi, 2)], r3u.at[h, qi],
+                    q_s.at[UP, h, qi, 0], q_r.at[UP, h, qi, 0], hdev(h, 0, d),
+                )
+
+    def us3():
+        own = pl.ds(6, 2)
+        for h in range(2):
+            for qi in range(3):
+                got(r3u.at[h, qi], q_s.at[UP, h, qi, 0], q_r.at[UP, h, qi, 0])
+            v = sfu[h, 1, own]
+            for qi in range(3):
+                v = v + r3u[h, qi, 1].astype(F32)
+            finu[h] = v
+            send(finu.at[h], rfu.at[h], f_s.at[UP, h], f_r.at[UP, h], mate)
+            v = sfu[h, 0, own]
+            for qi in range(3):
+                v = v + r3u[h, qi, 0].astype(F32)
+            ug_o[pl.ds(2 * h, 2), mine, :] = v
+
     def tabsend():
         send(tab, tabp, t_s.at[2], t_r.at[2], mate)
 
@@ -447,72 +522,66 @@
                 cp.wait()
 
     plan = (
-        (ag1, UP),
-        (ag1p, UP),
+        (upq,),
         (tabsend,),
+        (ag1, DOWN),
         (landed, 4, 6),
         (zpart, 0),
         (zsend, 0, 0),
         (zsend, 0, 1),
-        (ag2, UP),
-        (ag1, DOWN),
+        (upp,),
+        (ag1p, DOWN),
+        (ag2, DOWN),
         (landed, 5),
         (tables,),
-        (ag3, UP),
-        (ag1p, DOWN),
-        (ag4, UP),
+        (upd,),
+        (ag3, DOWN),
         (zsend, 1, 0),
-        (ag2, DOWN),
-        (zsend, 1, 1),
-        (ag5, UP),
-        (ag3, DOWN),
-        (zpart, 1),
         (ag6, UP),
         (arsend, UP),
+        (zsend, 1, 1),
+        (zpart, 1),
         (zsend, 2, 0),
+        (arsum, UP),
+        (ag4, DOWN),
         (zsend, 2, 1),
-        (ag4, DOWN),
-        (arsum, UP),
-        (zsend, 3, 0),
         (zpart, 2),
-        (zsend, 3, 1),
         (argot, UP),
         (terms, DOWN),
+        (zsend, 3, 0),
         (ag5, DOWN),
-        (zsend, 4, 0),
+        (zsend, 3, 1),
         (tgot, DOWN),
         (rs1far, DOWN, TWO_Q, 0),
-        (zsend, 4, 1),
+        (rs1far, DOWN, TWO_Q, 1),
         (ag6, DOWN),
         (arsend, DOWN),
-        (rs1far, DOWN, TWO_Q, 1),
+        (zsend, 4, 0),
         (rs1near, DOWN, TWO_Q, 0),
-        (zsend, 5, 0),
+        (zsend, 4, 1),
         (rs1near, DOWN, TWO_Q, 1),
-        (zsend, 5, 1),
+        (zpart, 3),
         (arsum, DOWN),
-        (zpart, 3),
         (rs2, DOWN, TWO_Q, 0),
         (rs2, DOWN, TWO_Q, 1),
-        (zsend, 6, 0),
-        (zsend, 6, 1),
+        (zsend, 5, 0),
+        (zsend, 5, 1),
         (rs3, DOWN),
         (argot, DOWN),
         (terms, UP),
         (rs4, DOWN, TWO_Q, 0),
         (tgot, UP),
-        (rs1far, UP, ALL_Q, 0),
-        (rs1near, UP, ALL_Q, 0),
+        (us1,),
+        (zsend, 6, 0),
         (rs4, DOWN, TWO_Q, 1),
-        (rs3, UP),
-        (rs2, UP, ALL_Q, 0),
+        (zsend, 6, 1),
         (rs5, DOWN),
-        (zlast,),
-        (rs4, UP, ALL_Q, 0),
+        (us2,),
+        (zlast, 0),
+        (zlast, 1),
         (rs6, DOWN),
-        (rs5, UP),
+        (us3,),
         (rs7, DOWN),
-        (rs6, UP),
         (rs7, UP),
     )
     for act, *details in plan:
@@ -572,12 +641,14 @@
             pltpu.SMEM((2, 8, 128), jnp.int32),
             pltpu.SMEM((tiles,), jnp.int32),
             *pair(hrank, (2, 4, 2, 8), BF),
-            *pair(hrank, (2, 2, 8), BF),
-            *pair(hrank, (2, 2, 2, 8), BF),
+            vm((2, 3, 2, 8, hrank, feat), BF),
+            vm((2, 2, 8, hrank, width), BF),
+            vm((2, 2, 2, 8, hrank, width), BF),
             *pair(hrank, (2, 2, 8), F32),
             *pair(hrank, (2, 2, 8), BF),
-            *pair(hrank, (2, 2, 2), BF),
-            *pair(hrank, (2, 2, 2, 2), BF),
+            vm((2, 3, 2, 2, hrank, feat), BF),
+            vm((2, 2, 2, hrank, width), BF),
+            vm((2, 2, 2, 2, hrank, width), BF),
             *pair(hrank, (2, 2), F32),
             *pair(hrank, (2, 2), F32),
             dma((8 + NZ + 1,)),

time: 89.9 us -> 78.4 us (0.87)
  Pallas kernels: 89.1 us -> 77.6 us
    pallas_call x1, Pallas kernels: 87 us -> 75.5 us  [body(): pl.pallas_call(kernel, out_shape=shapes, in_specs=[pl.BlockSpec(memory_sp...]
where the time goes in v4:
time: 78.4 us; the launch traced here: 78.2 us
  Pallas kernels  77.6 us (99%)
    pallas_call x1, Pallas kernels, body(): pl.pallas_call(kernel, out_shape=shapes, in_specs=[pl.BlockSpec(memory_sp...  75.5 us
    pallas_call x1, Pallas kernels, body(): pl.pallas_call(place, out_shape=shapes, in_specs=[vmem] * 3, out_specs=(v...  2.08 us

profile of v4, /device:TPU:1, one launch (start us, length us, event | category | flops | bytes accessed | tf_op | source)
XLA Modules:
  0.0 78.2 jit_solution(4873226572293087683)
XLA Ops:
  0.6 75.5 %adapters_and_projection.1 = (bf16[2048,128]{1,0:T(8,128)(2,1)}, f32[4,32,640]{2,1,0:T(8,128)}, f32[4,32,128]{2,1,0:T(8,128)}) custom-call(s32[16]{0:T(128)} %ids.1, bf16[2048,640]{1,0:T(8,128)(2,1)} %tok_h.1, bf16[640,1024]{1,0:T(8,128)(2,1)} %w_h.1, bf16[4,32,640]{2,1,0:T(8,128)(2,1)} %down_h.1, bf16[4,32,128]{2,1,0:T(8,128)(2,1)} %up_h.1, ...), custom_call_target="tpu_custom_call" | custom-call | tf_op jit(solution)/shard_map/adapters_and_projection/pallas_call | solution.py:621
  76.1 2.1 %place_results.1 = (bf16[2048,128]{1,0:T(8,128)(2,1)}, f32[4,32,640]{2,1,0:T(8,128)}, f32[4,32,128]{2,1,0:T(8,128)}) custom-call(bf16[2048,128]{1,0:T(8,128)(2,1)} %get-tuple-element.6.val_i, f32[4,32,640]{2,1,0:T(8,128)} %get-tuple-element.7.gd_i, f32[4,32,128]{2,1,0:T(8,128)} %get-tuple-element.8.ug_i), custom_call_target="tpu_custom_call" | custom-call | tf_op jit(solution)/shard_map/place_results/pallas_call | solution.py:679

commit v5 on v4

--- a/solution.py
+++ b/solution.py
@@ -527,9 +527,9 @@
         (ag1, DOWN),
         (landed, 4, 6),
         (zpart, 0),
+        (upp,),
         (zsend, 0, 0),
         (zsend, 0, 1),
-        (upp,),
         (ag1p, DOWN),
         (ag2, DOWN),
         (landed, 5),
@@ -541,14 +541,14 @@
         (arsend, UP),
         (zsend, 1, 1),
         (zpart, 1),
+        (arsum, UP),
         (zsend, 2, 0),
-        (arsum, UP),
         (ag4, DOWN),
         (zsend, 2, 1),
         (zpart, 2),
         (argot, UP),
+        (zsend, 3, 0),
         (terms, DOWN),
-        (zsend, 3, 0),
         (ag5, DOWN),
         (zsend, 3, 1),
         (tgot, DOWN),
@@ -556,8 +556,8 @@
         (rs1far, DOWN, TWO_Q, 1),
         (ag6, DOWN),
         (arsend, DOWN),
+        (rs1near, DOWN, TWO_Q, 0),
         (zsend, 4, 0),
-        (rs1near, DOWN, TWO_Q, 0),
         (zsend, 4, 1),
         (rs1near, DOWN, TWO_Q, 1),
         (zpart, 3),

time: 78.4 us -> 78.4 us (level)
  no operation moved by 1% of the time
where the time goes in v5:
time: 78.4 us; the launch traced here: 78.2 us
  Pallas kernels  77.6 us (99%)
    pallas_call x1, Pallas kernels, body(): pl.pallas_call(kernel, out_shape=shapes, in_specs=[pl.BlockSpec(memory_sp...  75.5 us
    pallas_call x1, Pallas kernels, body(): pl.pallas_call(place, out_shape=shapes, in_specs=[vmem] * 3, out_specs=(v...  2.08 us

profile of v5, /device:TPU:1, one launch (start us, length us, event | category | flops | bytes accessed | tf_op | source)
XLA Modules:
  0.0 78.2 jit_solution(9930336523669275531)
XLA Ops:
  0.6 75.5 %adapters_and_projection.1 = (bf16[2048,128]{1,0:T(8,128)(2,1)}, f32[4,32,640]{2,1,0:T(8,128)}, f32[4,32,128]{2,1,0:T(8,128)}) custom-call(s32[16]{0:T(128)} %ids.1, bf16[2048,640]{1,0:T(8,128)(2,1)} %tok_h.1, bf16[640,1024]{1,0:T(8,128)(2,1)} %w_h.1, bf16[4,32,640]{2,1,0:T(8,128)(2,1)} %down_h.1, bf16[4,32,128]{2,1,0:T(8,128)(2,1)} %up_h.1, ...), custom_call_target="tpu_custom_call" | custom-call | tf_op jit(solution)/shard_map/adapters_and_projection/pallas_call | solution.py:621
  76.1 2.1 %place_results.1 = (bf16[2048,128]{1,0:T(8,128)(2,1)}, f32[4,32,640]{2,1,0:T(8,128)}, f32[4,32,128]{2,1,0:T(8,128)}) custom-call(bf16[2048,128]{1,0:T(8,128)(2,1)} %get-tuple-element.6.val_i, f32[4,32,640]{2,1,0:T(8,128)} %get-tuple-element.7.gd_i, f32[4,32,128]{2,1,0:T(8,128)} %get-tuple-element.8.ug_i), custom_call_target="tpu_custom_call" | custom-call | tf_op jit(solution)/shard_map/place_results/pallas_call | solution.py:679
